TPU v7x, 256 devices: a whole 4x4x8 slice. The times are simulated.
256 devices in a mesh: seq: 32 (over z, x), tp: 8 (over y, core).
Axes of the slice: x: 4, y: 4, z: 8, core: 2. Of those that a mesh axis runs over, the one named last changes fastest.
Arguments:
- hidden_new: bfloat16 [3, 16, 8192], P(None, None, 'seq'), may hold values from -6 to 6
- w_kv: bfloat16 [8192, 8, 256], P('seq', 'tp'), may hold values from -0.0625 to 0.0625
- w_out: bfloat16 [8192, 8192], P('tp', 'seq'), may hold values from -0.0625 to 0.0625
- queries_draft: bfloat16 [3, 4, 8, 32, 128], P(None, None, 'tp'), may hold values from -48 to 48
- queries_verify: bfloat16 [3, 4, 8, 32, 128], P(None, None, 'tp'), may hold values from -48 to 48
- keys_cache: bfloat16 [4, 8, 65536, 128], P(None, 'tp', 'seq'), may hold values from -6 to 6
- values_cache: bfloat16 [4, 8, 65536, 128], P(None, 'tp', 'seq'), may hold values from -6 to 6
- key_levels: bfloat16 [4, 8, 65536, 128], P(None, 'tp', 'seq'), may hold values from -8 to 7, as said below
- value_levels: bfloat16 [4, 8, 65536, 128], P(None, 'tp', 'seq'), may hold values from -8 to 7, as said below
- key_scales: float32 [4, 8, 65536], P(None, 'tp', 'seq'), may hold values from 0.05 to 0.5
- value_scales: float32 [4, 8, 65536], P(None, 'tp', 'seq'), may hold values from 0.1 to 0.4
- lengths: int32 [4], replicated, may hold values from 2 to 65528, as said below
- accepted: int32 [2, 4], replicated, may hold values from 0 to 4, as said below
Outputs:
- layer_out: bfloat16 [3, 2, 16, 8192], P(None, None, None, 'seq')
Inputs may be any that keep to these rules, and one draw needn't show every extreme that they name: `key_levels`: every entry is a whole number. Positions 0 and 1 of every sequence and head hold equal levels. `value_levels`: every entry is a whole number. `lengths`: some sequence starts with exactly 65528 valid positions, another with 16 or fewer. `accepted`: the values 0 and 4 both occur.
All inputs are finite; a program needn't handle non-finite values.
Results may differ from a plain program's by a relative error of at most 0.006.
The roundings to bfloat16 on the way count: a program that leaves them out, or rounds other values in their place, can miss the bound.
Values may be sent and summed in bfloat16 or wider, within the bound.
No kernel may reach another device: no remote copies, remote signals or barrier semaphores. Data moves between devices by JAX's collectives and lax.ppermute only.
A program may use at most 128 MiB of HBM per device.

v0:
```python
import math

import jax
import jax.numpy as jnp
from jax import lax
from jax.sharding import Mesh
from jax.sharding import PartitionSpec as P

HD = 128
GROUP = 8
R = 4
ROUNDS = 3
SEQ = ("seq_0", "seq_1")


NEG = -1e30


def one_axis_at_a_time(shard, axes):
    for axis in axes:
        shard = lax.psum(shard, axis)
    return shard


def all_in_one(shard, axis):
    leaves = jax.tree.leaves(shard)
    sequence = sorted(range(len(leaves)), key=lambda k: -leaves[k].size)
    width = (1, *leaves[sequence[0]].shape)[-1]
    lines = [
        jnp.pad(leaves[k].reshape(-1), (0, -leaves[k].size % width)).reshape(-1, width)
        for k in sequence
    ]
    both, at, found = (lax.all_gather(jnp.concatenate(lines), axis), 0, {})
    for k, line in zip(sequence, lines):
        slab = both[:, at : at + len(line)].reshape(len(both), -1)
        found[k] = slab[:, : leaves[k].size].reshape(-1, *leaves[k].shape)
        at += len(line)
    numbers = iter(range(len(leaves)))
    return jax.tree.map(lambda _: found[next(numbers)], shard)


def combined_by_axis(shard, axes, combine):
    for axis in axes:
        pieces = all_in_one(shard, axis)
        shard = jax.tree.map(lambda part: part[0], pieces)
        for k in range(1, lax.axis_size(axis)):
            shard = combine(shard, jax.tree.map(lambda part: part[k], pieces))
    return shard


def sent_to_all(shard, axis):
    peers = lax.axis_size(axis)
    return lax.all_to_all(
        jnp.broadcast_to(shard[None], (peers, *shard.shape)), axis, 0, 0, tiled=True
    )


def over_copies(shard, axis):
    return sent_to_all(shard, axis).sum(axis=0)


def dequantize(levels, scales):
    return (levels.astype(jnp.float32) * scales[..., None]).astype(jnp.bfloat16)


def attend(queries, keys, values, usable):
    scores = jnp.einsum("bhqd,bhkd->bhqk", queries, keys, preferred_element_type=jnp.float32) * (
        1.0 / math.sqrt(HD)
    )
    scores = jnp.where(usable, scores, NEG)
    maxima = jnp.max(scores, axis=-1)
    weights = jnp.where(usable, jnp.exp(scores - maxima[..., None]), 0.0).astype(jnp.bfloat16)
    totals = jnp.sum(weights.astype(jnp.float32), axis=-1)
    weighted = jnp.einsum("bhqk,bhkd->bhqd", weights, values, preferred_element_type=jnp.float32)
    return (maxima, totals, weighted)


def combine(former, latter):
    highest = jnp.maximum(former[0], latter[0])
    former_w = jnp.exp(former[0] - highest)
    latter_w = jnp.exp(latter[0] - highest)
    return (
        highest,
        former[1] * former_w + latter[1] * latter_w,
        former[2] * former_w[..., None] + latter[2] * latter_w[..., None],
    )


def merge_pair(former, latter):
    return combine(former[:3], latter[:3]) + combine(former[3:], latter[3:])


def finish(partial_value):
    return (partial_value[2] / partial_value[1][..., None]).astype(jnp.bfloat16)


def arrange(attended):
    kind_count, batch_size, head_count, query_rows, head_width = attended.shape
    split_rows = attended.reshape(kind_count, batch_size, head_count, GROUP, R, head_width)
    return split_rows.transpose(0, 1, 4, 2, 3, 5).reshape(
        kind_count * batch_size * R, head_count * GROUP * head_width
    )


def per_device(
    hidden_new,
    w_kv,
    w_out,
    queries_draft,
    queries_verify,
    keys_cache,
    values_cache,
    key_levels,
    value_levels,
    key_scales,
    value_scales,
    lengths,
    accepted,
):
    batch_size, head_count, local_len, head_width = keys_cache.shape
    seq_index = lax.axis_index(SEQ)
    first_row = seq_index * local_len
    key_low = dequantize(key_levels, key_scales)
    value_low = dequantize(value_levels, value_scales)
    places = first_row + jnp.arange(local_len, dtype=jnp.int32)
    stored = (places[None, :] < lengths[:, None])[:, None, :, None]
    flat_kv = w_kv.reshape(w_kv.shape[0], -1)
    tokens = jnp.arange(GROUP * R, dtype=jnp.int32) % R
    causal = (tokens[:, None] >= jnp.arange(R, dtype=jnp.int32)[None, :])[None, None]
    offsets = jnp.arange(R, dtype=jnp.int32)[None, :]
    batch_rows = jnp.broadcast_to(jnp.arange(batch_size, dtype=jnp.int32)[:, None], (batch_size, R))
    length_now = lengths
    results = []
    for turn_index in range(ROUNDS):
        partial_kv = jnp.dot(hidden_new[turn_index], flat_kv, preferred_element_type=jnp.float32)
        fresh_rows = (
            one_axis_at_a_time(partial_kv, SEQ)
            .astype(jnp.bfloat16)
            .reshape(batch_size, R, head_count, 2, head_width)
        )
        new_keys = fresh_rows[:, :, :, 0].transpose(0, 2, 1, 3)
        new_values = fresh_rows[:, :, :, 1].transpose(0, 2, 1, 3)
        usable = (places[None, :] < length_now[:, None])[:, None, None, :]
        draft_q = queries_draft[turn_index]
        verify_q = queries_verify[turn_index]
        draft_keys = jnp.where(stored, key_low, keys_cache)
        draft_values = jnp.where(stored, value_low, values_cache)
        draft_part = attend(draft_q, draft_keys, draft_values, usable)
        draft_self = attend(draft_q, new_keys, new_values, causal)
        verify_part = attend(verify_q, keys_cache, values_cache, usable)
        verify_self = attend(verify_q, new_keys, new_values, causal)
        joined = combined_by_axis(draft_part + verify_part, SEQ, merge_pair)
        attended = jnp.stack(
            [finish(combine(joined[:3], draft_self)), finish(combine(joined[3:], verify_self))]
        )
        projected = jnp.dot(arrange(attended), w_out, preferred_element_type=jnp.float32)
        summed = over_copies(projected, "tp")
        results.append(summed.astype(jnp.bfloat16).reshape(2, batch_size * R, -1))
        if turn_index + 1 < ROUNDS:
            accepted_now = accepted[turn_index]
            targets = length_now[:, None] + offsets - first_row
            landing = (offsets < accepted_now[:, None]) & (targets >= 0) & (targets < local_len)
            targets = jnp.where(landing, targets, local_len)
            keys_cache = keys_cache.at[batch_rows, :, targets, :].set(
                fresh_rows[:, :, :, 0], mode="drop"
            )
            values_cache = values_cache.at[batch_rows, :, targets, :].set(
                fresh_rows[:, :, :, 1], mode="drop"
            )
            length_now = length_now + accepted_now
    return jnp.stack(results)


def solution(mesh):
    finer = Mesh(mesh.devices.reshape(8, 4, mesh.shape["tp"]), ("seq_0", "seq_1", "tp"))
    in_specs = (
        P(None, None, SEQ),
        P(SEQ, "tp", None),
        P("tp", SEQ),
        P(None, None, "tp", None, None),
        P(None, None, "tp", None, None),
        P(None, "tp", SEQ, None),
        P(None, "tp", SEQ, None),
        P(None, "tp", SEQ, None),
        P(None, "tp", SEQ, None),
        P(None, "tp", SEQ),
        P(None, "tp", SEQ),
        P(),
        P(),
    )
    out_specs = P(None, None, None, SEQ)
    return jax.shard_map(
        per_device, mesh=finer, in_specs=in_specs, out_specs=out_specs, check_vma=False
    )
```

profile of v0, /device:TPU:1, one launch (start us, length us, event | category | flops | bytes accessed | tf_op | source)
XLA Modules:
  0.0 246.7 jit_solution(1245604594678080687)
XLA Ops:
  6.5 3.2 %copy.147 = bf16[4,1,2048,128]{3,2,1,0:T(8,128)(2,1)} copy(bf16[4,1,2048,128]{3,2,1,0:T(8,128)(2,1)} %param.18) | data formatting | bytes 4194304
  10.7 3.4 %fusion.503 = (f32[4,32]{1,0:T(4,128)S(1)}, f32[4,32,2048]{2,1,0:T(8,128)}) fusion(bf16[4,1,2048,128]{3,2,1,0:T(8,128)(2,1)} %copy.147, bf16[3,4,1,32,128]{4,3,1,2,0:T(8,128)(2,1)S(1)} %bitcast.2226, pred[4,2048]{1,0:T(4,128)(4,1)S(1)} %get-tuple-element.321), kind=kOutput, calls=%fused_computation.991 | convolution fusion | flops 67895168 | bytes 3187200 | tf_op jit(solution)/shard_map/bhqd,bhkd->bhqk/dot_general | solution.py:67
  14.1 5.3 %fusion.502 = (f32[4,32]{1,0:T(4,128)S(1)}, f32[4,32,2048]{2,1,0:T(8,128)}) fusion(bf16[3,4,1,32,128]{4,3,1,2,0:T(8,128)(2,1)S(1)} %bitcast.2278, bf16[4,1,2048,128]{3,2,1,0:T(8,128)(2,1)S(1)} %copy-done.1, pred[4,2048]{1,0:T(4,128)(4,1)S(1)} %get-tuple-element.321, f32[4,2048]{1,0:T(4,128)S(1)} %bitcast.2262, bf16[4,1,2048,128]{3,2,1,0:T(8,128)(2,1)} %param.20), kind=kOutput, calls=%fused_computation.990 | convolution fusion | flops 72089472 | bytes 5325312 | tf_op jit(solution)/shard_map/bhqd,bhkd->bhqk/dot_general | solution.py:67
  24.1 3.0 %fusion.19 = f32[4,32,128]{2,1,0:T(8,128)S(1)} fusion(bf16[4,1,2048,128]{3,2,1,0:T(8,128)(2,1)S(1)} %copy.148, pred[4,2048]{1,0:T(4,128)(4,1)S(1)} %get-tuple-element.321, bf16[4,1,2048,128]{3,2,1,0:T(8,128)(2,1)S(1)} %copy-done.13, f32[4,2048]{1,0:T(4,128)S(1)} %bitcast.2265, f32[4,32,2048]{2,1,0:T(8,128)S(1)} %copy-done.6, f32[4,32]{1,0:T(4,128)S(1)} %get-tuple-element.330), kind=kOutput, calls=%fused_computation.34 | convolution fusion | flops 72089600 | bytes 5349888 | tf_op jit(solution)/shard_map/bhqk,bhkd->bhqd/dot_general | solution.py:74
  29.4 27.5 %all-reduce = (f32[16,256]{1,0:T(8,128)S(1)}, f32[16,256]{1,0:T(8,128)S(1)}, f32[16,256]{1,0:T(8,128)S(1)}) all-reduce(f32[16,256]{1,0:T(8,128)S(1)} %fusion.64, f32[16,256]{1,0:T(8,128)S(1)} %fusion.62, f32[16,256]{1,0:T(8,128)S(1)} %fusion.60), channel_id=1, replica_groups=mesh['seq_0'=8,'seq_1'=4,'tp'=8] {'seq_0'}, use_global_device_ids=true, to_apply=%region_4.5 | all-reduce | flops 12288 | bytes 98304 | tf_op jit(solution)/shard_map/psum | solution.py:21
  57.0 14.2 %all-reduce.1 = (bf16[16,256]{1,0:T(8,128)(2,1)S(1)}, bf16[16,256]{1,0:T(8,128)(2,1)S(1)}, bf16[16,256]{1,0:T(8,128)(2,1)S(1)}) all-reduce(f32[16,256]{1,0:T(8,128)S(1)} %get-tuple-element.65, f32[16,256]{1,0:T(8,128)S(1)} %get-tuple-element.66, f32[16,256]{1,0:T(8,128)S(1)} %get-tuple-element.67), channel_id=1, replica_groups=mesh['seq_0'=8,'seq_1'=4,'tp'=8] {'seq_1'}, use_global_device_ids=true, to_apply=%region_5.6 | all-reduce | flops 12288 | bytes 73728 | tf_op jit(solution)/shard_map/psum | solution.py:21
  71.4 2.4 scatter_fusion
  73.8 5.6 %fusion.504 = (f32[4,32]{1,0:T(4,128)S(1)}, f32[4,32,2048]{2,1,0:T(8,128)}) fusion(bf16[3,4,1,32,128]{4,3,1,2,0:T(8,128)(2,1)S(1)} %bitcast.2279, bf16[4,2048,128]{2,1,0:T(8,128)(2,1)} %scatter_fusion, pred[4,2048]{1,0:T(4,128)(4,1)S(1)} %get-tuple-element.321, f32[4,2048]{1,0:T(4,128)S(1)} %bitcast.2263, bf16[4,1,2048,128]{3,2,1,0:T(8,128)(2,1)} %param.20, ...), kind=kOutput, calls=%fused_computation.992 | convolution fusion | flops 72089472 | bytes 5325312 | tf_op jit(solution)/shard_map/bhqd,bhkd->bhqk/dot_general | solution.py:67
  79.4 3.4 %fusion.505 = (f32[4,32]{1,0:T(4,128)S(1)}, f32[4,32,2048]{2,1,0:T(8,128)}) fusion(bf16[4,2048,128]{2,1,0:T(8,128)(2,1)} %scatter_fusion, bf16[3,4,1,32,128]{4,3,1,2,0:T(8,128)(2,1)S(1)} %bitcast.2227, pred[4,2048]{1,0:T(4,128)(4,1)S(1)} %get-tuple-element.319), kind=kOutput, calls=%fused_computation.993 | convolution fusion | flops 67895168 | bytes 3187200 | tf_op jit(solution)/shard_map/bhqd,bhkd->bhqk/dot_general | solution.py:67
  88.8 3.0 %fusion.16 = f32[4,32,128]{2,1,0:T(8,128)S(1)} fusion(bf16[4,2048,128]{2,1,0:T(8,128)(2,1)S(1)} %scatter_fusion.1, pred[4,2048]{1,0:T(4,128)(4,1)S(1)} %get-tuple-element.321, bf16[4,1,2048,128]{3,2,1,0:T(8,128)(2,1)S(1)} %copy-done.14, f32[4,2048]{1,0:T(4,128)S(1)} %bitcast.2266, f32[4,32,2048]{2,1,0:T(8,128)S(1)} %copy-done.5, ...), kind=kOutput, calls=%fused_computation.29 | convolution fusion | flops 72089600 | bytes 5358080 | tf_op jit(solution)/shard_map/bhqk,bhkd->bhqd/dot_general | solution.py:74
  94.0 2.4 scatter_fusion.2
  96.4 5.6 %fusion.506 = (f32[4,32]{1,0:T(4,128)S(1)}, f32[4,32,2048]{2,1,0:T(8,128)}) fusion(bf16[3,4,1,32,128]{4,3,1,2,0:T(8,128)(2,1)S(1)} %bitcast.2280, bf16[4,2048,128]{2,1,0:T(8,128)(2,1)} %scatter_fusion.2, pred[4,2048]{1,0:T(4,128)(4,1)S(1)} %get-tuple-element.321, f32[4,2048]{1,0:T(4,128)S(1)} %bitcast.2264, bf16[4,1,2048,128]{3,2,1,0:T(8,128)(2,1)} %param.20, ...), kind=kOutput, calls=%fused_computation.994 | convolution fusion | flops 72089472 | bytes 5325312 | tf_op jit(solution)/shard_map/bhqd,bhkd->bhqk/dot_general | solution.py:67
  102.1 3.4 %fusion.507 = (f32[4,32]{1,0:T(4,128)S(1)}, f32[4,32,2048]{2,1,0:T(8,128)}) fusion(bf16[4,2048,128]{2,1,0:T(8,128)(2,1)} %scatter_fusion.2, bf16[3,4,1,32,128]{4,3,1,2,0:T(8,128)(2,1)S(1)} %bitcast.2228, pred[4,2048]{1,0:T(4,128)(4,1)S(1)} %get-tuple-element.320), kind=kOutput, calls=%fused_computation.995 | convolution fusion | flops 67895168 | bytes 3187200 | tf_op jit(solution)/shard_map/bhqd,bhkd->bhqk/dot_general | solution.py:67
  111.5 3.0 %fusion.12 = f32[4,32,128]{2,1,0:T(8,128)S(1)} fusion(bf16[4,2048,128]{2,1,0:T(8,128)(2,1)S(1)} %scatter_fusion.3, pred[4,2048]{1,0:T(4,128)(4,1)S(1)} %get-tuple-element.321, bf16[4,1,2048,128]{3,2,1,0:T(8,128)(2,1)S(1)} %copy-done.15, f32[4,2048]{1,0:T(4,128)S(1)} %bitcast.2267, f32[4,32,2048]{2,1,0:T(8,128)S(1)} %copy-done.4, ...), kind=kOutput, calls=%fused_computation.25 | convolution fusion | flops 72089600 | bytes 5358080 | tf_op jit(solution)/shard_map/bhqk,bhkd->bhqd/dot_general | solution.py:74
  119.7 15.0 %all-gather.18.cloned.1.call-done = f32[8,260,128]{2,1,0:T(8,128)} async-done(((f32[1,260,128]{2,1,0:T(8,128)}), f32[8,260,128]{2,1,0:T(8,128)}) %all-gather.18.cloned.1.call-update) | async-done | bytes 1064976 | tf_op jit(solution)/shard_map/all_gather | solution.py:33
  149.9 11.2 %all-gather.7 = f32[4,260,128]{2,1,0:T(8,128)S(1)} all-gather(f32[1,260,128]{2,1,0:T(8,128)S(1)} %bitcast.2217), channel_id=3, replica_groups=mesh['seq_0'=8,'seq_1'=4,'tp'=8] {'seq_1'}, dimensions={0}, use_global_device_ids=true | all-gather | bytes 665600 | tf_op jit(solution)/shard_map/all_gather | solution.py:33
  161.1 10.7 %all-gather.9 = f32[4,260,128]{2,1,0:T(8,128)S(1)} all-gather(f32[1,260,128]{2,1,0:T(8,128)S(1)} %bitcast.2218), channel_id=5, replica_groups=mesh['seq_0'=8,'seq_1'=4,'tp'=8] {'seq_1'}, dimensions={0}, use_global_device_ids=true | all-gather | bytes 665600 | tf_op jit(solution)/shard_map/all_gather | solution.py:33
  181.7 10.4 %all-gather.11 = f32[4,260,128]{2,1,0:T(8,128)S(1)} all-gather(f32[1,260,128]{2,1,0:T(8,128)S(1)} %bitcast.2219), channel_id=7, replica_groups=mesh['seq_0'=8,'seq_1'=4,'tp'=8] {'seq_1'}, dimensions={0}, use_global_device_ids=true | all-gather | bytes 665600 | tf_op jit(solution)/shard_map/all_gather | solution.py:33
  195.2 14.6 %all-to-all-start = ((f32[8,32,256]{2,1,0:T(8,128)}), f32[8,32,256]{2,1,0:T(8,128)S(1)}, u32[]{:S(2)}, u32[]{:S(2)}) async-start(f32[8,32,256]{2,1,0:T(8,128)} %broadcast_in_dim.195), calls=%async_computation | async-start | bytes 524288 | tf_op jit(solution)/shard_map/all_to_all | solution.py:53
  213.9 2.4 all-to-all-done
  217.0 4.4 %all-to-all-start.1 = ((f32[8,32,256]{2,1,0:T(8,128)}), f32[8,32,256]{2,1,0:T(8,128)S(1)}, u32[]{:S(2)}, u32[]{:S(2)}) async-start(f32[8,32,256]{2,1,0:T(8,128)} %broadcast_in_dim.199), calls=%async_computation.1 | async-start | bytes 524288 | tf_op jit(solution)/shard_map/all_to_all | solution.py:53
  221.6 6.3 %all-to-all-done.1 = f32[8,32,256]{2,1,0:T(8,128)S(1)} async-done(((f32[8,32,256]{2,1,0:T(8,128)}), f32[8,32,256]{2,1,0:T(8,128)S(1)}, u32[]{:S(2)}, u32[]{:S(2)}) %all-to-all-start.1) | async-done | bytes 262176 | tf_op jit(solution)/shard_map/all_to_all | solution.py:53
  228.6 4.4 %all-to-all-start.2 = ((f32[8,32,256]{2,1,0:T(8,128)}), f32[8,32,256]{2,1,0:T(8,128)S(1)}, u32[]{:S(2)}, u32[]{:S(2)}) async-start(f32[8,32,256]{2,1,0:T(8,128)} %broadcast_in_dim.203), calls=%async_computation.2 | async-start | bytes 524288 | tf_op jit(solution)/shard_map/all_to_all | solution.py:53
  233.0 6.5 %all-to-all-done.2 = f32[8,32,256]{2,1,0:T(8,128)S(1)} async-done(((f32[8,32,256]{2,1,0:T(8,128)}), f32[8,32,256]{2,1,0:T(8,128)S(1)}, u32[]{:S(2)}, u32[]{:S(2)}) %all-to-all-start.2) | async-done | bytes 262176 | tf_op jit(solution)/shard_map/all_to_all | solution.py:53
  (215 shorter events, 61.8 us)
Async XLA Ops:
  6.5 187.7 %copy-start = (bf16[1024,256]{1,0:T(8,128)(2,1)S(1)}, bf16[1024,256]{1,0:T(8,128)(2,1)}, u32[]{:S(2)}) copy-start(bf16[1024,256]{1,0:T(8,128)(2,1)} %param.15) | copy-start | bytes 1572868
  6.5 110.8 %all-gather.16.cloned.1.call-start = ((), (), s32[]{:S(2)}) async-start(), calls=%async_computation.3 | async-start | bytes 1216512 | tf_op jit(solution)/shard_map/all_gather | solution.py:33
  6.5 3.2 %copy-start.2 = (bf16[4,1,2048,128]{3,2,1,0:T(8,128)(2,1)S(1)}, bf16[4,1,2048,128]{3,2,1,0:T(8,128)(2,1)}, u32[]{:S(2)}) copy-start(bf16[4,1,2048,128]{3,2,1,0:T(8,128)(2,1)} %param.19) | copy-start | bytes 6291460
  9.8 0.8 copy-start.8
  9.8 0.8 copy-start.11
  9.8 0.8 copy-start.12
  9.8 0.9 copy-start.7
  9.9 4.2 %copy-start.16 = (bf16[3,4,1,32,128]{4,3,2,1,0:T(8,128)(2,1)S(1)}, bf16[3,4,1,32,128]{4,3,2,1,0:T(8,128)(2,1)}, u32[]{:S(2)}) copy-start(bf16[3,4,1,32,128]{4,3,2,1,0:T(8,128)(2,1)} %param.16) | copy-start | bytes 294916
  10.0 4.2 %copy-start.1 = (bf16[4,1,2048,128]{3,2,1,0:T(8,128)(2,1)S(1)}, bf16[4,1,2048,128]{3,2,1,0:T(8,128)(2,1)}, u32[]{:S(2)}) copy-start(bf16[4,1,2048,128]{3,2,1,0:T(8,128)(2,1)} %copy.147) | copy-start | bytes 6291460
  19.4 2.4 copy-start.9
  21.8 1.9 copy-start.6
  21.8 2.2 copy-start.13
  24.1 4.9 %copy-start.3 = (bf16[256,1,256]{2,0,1:T(8,128)(2,1)S(1)}, bf16[256,1,256]{2,0,1:T(8,128)(2,1)}, u32[]{:S(2)}) copy-start(bf16[256,1,256]{2,0,1:T(8,128)(2,1)} %param.14) | copy-start | bytes 393220
  24.1 4.9 %copy-start.10 = (bf16[3,16,256]{2,1,0:T(8,128)(2,1)S(1)}, bf16[3,16,256]{2,1,0:T(8,128)(2,1)}, u32[]{:S(2)}) copy-start(bf16[3,16,256]{2,1,0:T(8,128)(2,1)} %param.13) | copy-start | bytes 73732
  28.9 105.8 %all-gather.18.cloned.1.call-start = ((), (), s32[]{:S(2)}) async-start(), calls=%async_computation.4 | async-start | bytes 1216512 | tf_op jit(solution)/shard_map/all_gather | solution.py:33
  86.5 1.9 copy-start.5
  86.6 2.2 copy-start.14
  93.6 79.4 %all-gather.20.cloned.1.call-start = ((), (), s32[]{:S(2)}) async-start(), calls=%async_computation.5 | async-start | bytes 1216512 | tf_op jit(solution)/shard_map/all_gather | solution.py:33
  109.2 1.9 copy-start.4
  109.2 2.2 copy-start.15
  195.2 21.1 %all-to-all-start = ((f32[8,32,256]{2,1,0:T(8,128)}), f32[8,32,256]{2,1,0:T(8,128)S(1)}, u32[]{:S(2)}, u32[]{:S(2)}) async-start(f32[8,32,256]{2,1,0:T(8,128)} %broadcast_in_dim.195), calls=%async_computation | async-start | bytes 524288 | tf_op jit(solution)/shard_map/all_to_all | solution.py:53
  217.0 10.9 %all-to-all-start.1 = ((f32[8,32,256]{2,1,0:T(8,128)}), f32[8,32,256]{2,1,0:T(8,128)S(1)}, u32[]{:S(2)}, u32[]{:S(2)}) async-start(f32[8,32,256]{2,1,0:T(8,128)} %broadcast_in_dim.199), calls=%async_computation.1 | async-start | bytes 524288 | tf_op jit(solution)/shard_map/all_to_all | solution.py:53
  228.6 10.9 %all-to-all-start.2 = ((f32[8,32,256]{2,1,0:T(8,128)}), f32[8,32,256]{2,1,0:T(8,128)S(1)}, u32[]{:S(2)}, u32[]{:S(2)}) async-start(f32[8,32,256]{2,1,0:T(8,128)} %broadcast_in_dim.203), calls=%async_computation.2 | async-start | bytes 524288 | tf_op jit(solution)/shard_map/all_to_all | solution.py:53
Sparse Core Ops, SparseCore 0:
  29.0 38.5 all-gather.15
  93.8 40.9 all-gather.17
  136.6 36.4 all-gather.19
where the time goes:
time: 249 us; the launch traced here: 247 us
  blocking collectives  74 us (30%)
  matrix products  44.7 us (18%)
  other arithmetic  33.4 us (13%)
  waiting for transfers between devices  31.4 us (13%)
  local copies, waits for them, and re-layouts  25.8 us (10%)
  starting transfers between devices  23.6 us (9%)
  between operations  13.8 us (6%)
    psum x2, blocking collectives, one_axis_at_a_time(): shard = lax.psum(shard, axis)  41.7 us
    all_gather x3, blocking collectives, all_in_one(): both, at, found = (lax.all_gather(jnp.concatenate(lines), axis), 0, {})  32.3 us
    dot_general x12, matrix products, attend(): jnp.einsum('bhqd,bhkd->bhqk', queries, keys, preferred_element_type=jnp.f...  27.5 us
    all_to_all x3, starting transfers between devices, sent_to_all(): lax.all_to_all(jnp.broadcast_to(shard[None], (peers, *shard.shape)), axis...  23.3 us
    dot_general x12, matrix products, attend(): jnp.einsum('bhqk,bhkd->bhqd', weights, values, preferred_element_type=jnp...  16.2 us
    all_gather x3, waiting for transfers between devices, all_in_one(): both, at, found = (lax.all_gather(jnp.concatenate(lines), axis), 0, {})  16.1 us
    all_to_all x3, waiting for transfers between devices, sent_to_all(): lax.all_to_all(jnp.broadcast_to(shard[None], (peers, *shard.shape)), axis...  15.2 us
    exp x12, other arithmetic, combine(): latter_w = jnp.exp(latter[0] - highest)  8.52 us
  transfers between devices with their start and end apart: 6, of which 5 were waited for; matrix products, arithmetic and copies ran while one was open for 27% of the time, Pallas kernels for 0%

commit v1 on v0

v1 whole, which is shorter than its diff:
```python
import functools
import math

import jax
import jax.numpy as jnp
from jax import lax
from jax.experimental import pallas as pl
from jax.experimental.pallas import tpu as pltpu
from jax.sharding import PartitionSpec as P

HD = 128
GROUP = 8
R = 4
ROUNDS = 3
BATCH = 4
KINDS = 2
NEG = -1e30
SCALE = 1.0 / math.sqrt(HD)
SCALE_2 = SCALE / math.log(2.0)
ROWS = ROUNDS * GROUP * R
SHARE = KINDS * ROUNDS * R
NEW = ROUNDS * R
TOKENS = KINDS * ROUNDS * BATCH * R
AT_STATS = SHARE
AT_HIGH = SHARE + 8
AT_LOW = AT_HIGH + 2 * NEW
MESSAGE = AT_LOW + 2 * NEW
STEP = 512
VMEM_LIMIT = 48 * 1024 * 1024

f32 = jnp.float32
bf16 = jnp.bfloat16


def rounded(x):
    return x.astype(bf16).astype(f32)


def dot(a, b):
    return jnp.dot(a, b, preferred_element_type=f32)


def dot_rows(a, b):
    return lax.dot_general(a, b, (((1,), (1,)), ((), ())), preferred_element_type=f32)


def lanes_folded(x, op):
    folded = x[:, :128]
    for k in range(1, x.shape[1] // 128):
        folded = op(folded, x[:, k * 128 : (k + 1) * 128])
    return folded


def attend(queries, keys, values, usable, scores):
    positions = scores.shape[1]
    step = min(STEP, positions)
    steps = range(0, positions, step)
    highest = None
    for at in steps:
        part = dot_rows(queries, keys(at, step))
        lane = lax.broadcasted_iota(jnp.int32, (1, step), 1) + at
        part = part + jnp.where(lane < usable, 0.0, NEG)
        scores[:, at : at + step] = part
        folded = lanes_folded(part, jnp.maximum)
        highest = folded if highest is None else jnp.maximum(highest, folded)
    highest = jnp.max(highest, axis=1, keepdims=True)
    total = jnp.zeros((queries.shape[0], 128), f32)
    weighted = jnp.zeros((queries.shape[0], HD), f32)
    for at in steps:
        weights = jnp.exp2((scores[:, at : at + step] - highest) * SCALE_2).astype(bf16)
        total = total + lanes_folded(weights.astype(f32), jnp.add)
        weighted = weighted + dot(weights, values(at, step))
    return highest * SCALE, jnp.sum(total, axis=1, keepdims=True), weighted


def partials_kernel(
    lengths,
    hidden,
    w_kv,
    queries_draft,
    queries_verify,
    keys,
    values,
    key_levels,
    value_levels,
    key_scales,
    value_scales,
    message,
    scores,
    sums,
    stats,
    fresh,
    stage,
):
    b = pl.program_id(0)
    local_len = keys.shape[2]

    @pl.when(b == 0)
    def _():
        part = dot(hidden[...].reshape(ROUNDS * BATCH * R, hidden.shape[2]), w_kv[...])
        for k in range(BATCH):
            for kv in range(2):
                for t in range(ROUNDS):
                    fresh[k, kv * NEW + t * R : kv * NEW + (t + 1) * R] = part[
                        (t * BATCH + k) * R : (t * BATCH + k + 1) * R, kv * HD : (kv + 1) * HD
                    ]

    usable = jnp.clip(lengths[b] - lax.axis_index("seq") * local_len, 0, local_len)
    lane = lax.broadcasted_iota(jnp.int32, (ROWS, 128), 1)

    @pl.when(usable == 0)
    def _():
        sums[...] = jnp.zeros_like(sums)
        stats[...] = jnp.where(
            lax.broadcasted_iota(jnp.int32, stats.shape, 1) == 0, NEG, 0.0
        )

    @pl.when(usable > 0)
    def _():
        def expanded(levels, scales):
            columns = scales[0].T

            def rows(at, step):
                parts = [
                    (levels[0, 0, k : k + 128].astype(f32) * columns[:, k // 128 : k // 128 + 1]).astype(bf16)
                    for k in range(at, at + step, 128)
                ]
                return jnp.concatenate(parts, axis=0)

            return rows

        def plain(cache):
            return lambda at, step: cache[0, 0, at : at + step]

        draft = (queries_draft, expanded(key_levels, key_scales), expanded(value_levels, value_scales))
        verify = (queries_verify, plain(keys), plain(values))
        for kind, (queries, key_rows, value_rows) in enumerate((draft, verify)):
            rows = queries[...].reshape(ROWS, HD)
            maxima, totals, weighted = attend(rows, key_rows, value_rows, usable, scores.at[kind])
            sums[kind * ROWS : (kind + 1) * ROWS] = weighted
            stats[kind * ROWS : (kind + 1) * ROWS] = jnp.where(lane == 0, maxima, totals)

    pieces = [
        (g, kt * R, kt * GROUP * R + g * R) for g in range(GROUP) for kt in range(KINDS * ROUNDS)
    ]
    ordered = []
    for g, to, at in pieces:
        stage[g, to : to + R] = sums[at : at + R]
        ordered.append(stats[at : at + R])
    turned = jnp.concatenate(
        [jnp.concatenate(ordered, axis=0), jnp.zeros((256 - KINDS * ROWS, 128), f32)], axis=0
    ).T
    maxima, totals = turned[0:1], turned[1:2]
    parts = []
    for x in (maxima, totals):
        high = rounded(x)
        middle = rounded(x - high)
        parts += [high, middle, x - high - middle]
    parts = jnp.concatenate(parts + [jnp.zeros((2, 256), f32)], axis=0)
    high = rounded(fresh[b])
    low = fresh[b] - high
    for g in range(GROUP):
        stage[g, AT_STATS:AT_HIGH] = jnp.zeros((8, 128), f32)
        stage[g, AT_STATS:AT_HIGH, :SHARE] = parts[:, g * SHARE : (g + 1) * SHARE]
        stage[g, AT_HIGH:AT_LOW] = high
        stage[g, AT_LOW:] = low
    message[:, 0] = stage[...].astype(bf16)


def partials(hidden, w_kv, queries_draft, queries_verify, caches, scales, lengths):
    local_len = caches[0].shape[2]

    def whole(shape):
        return pl.BlockSpec(shape, lambda b, lengths: (0,) * len(shape))

    queries = pl.BlockSpec((ROUNDS, 1, 1, GROUP * R, HD), lambda b, lengths: (0, b, 0, 0, 0))
    cache = pl.BlockSpec((1, 1, local_len, HD), lambda b, lengths: (b, 0, 0, 0))
    scale = pl.BlockSpec((1, local_len // 128, 128), lambda b, lengths: (b, 0, 0))
    return pl.pallas_call(
        partials_kernel,
        out_shape=jax.ShapeDtypeStruct((GROUP, BATCH, MESSAGE, HD), bf16),
        grid_spec=pltpu.PrefetchScalarGridSpec(
            num_scalar_prefetch=1,
            grid=(BATCH,),
            in_specs=[whole(hidden.shape), whole(w_kv.shape), queries, queries]
            + [cache] * 4
            + [scale] * 2,
            out_specs=pl.BlockSpec((GROUP, 1, MESSAGE, HD), lambda b, lengths: (0, b, 0, 0)),
            scratch_shapes=[
                pltpu.VMEM((KINDS, ROWS, local_len), f32),
                pltpu.VMEM((KINDS * ROWS, HD), f32),
                pltpu.VMEM((KINDS * ROWS, 128), f32),
                pltpu.VMEM((BATCH, 2 * NEW, HD), f32),
                pltpu.VMEM((GROUP, MESSAGE, HD), f32),
            ],
        ),
        compiler_params=pltpu.CompilerParams(vmem_limit_bytes=VMEM_LIMIT),
        name="partials",
    )(lengths, hidden, w_kv, queries_draft, queries_verify, *caches, *scales)


def joined_kernel(accepted, received, queries_draft, queries_verify, copies):
    peers = received.shape[0]
    index = lax.axis_index("seq")
    g, b = index // BATCH, index % BATCH
    groups = [q[t, b, 0] for q in (queries_draft, queries_verify) for t in range(ROUNDS)]
    row = lax.broadcasted_iota(jnp.int32, (SHARE, KINDS * ROWS), 0)
    column = lax.broadcasted_iota(jnp.int32, (SHARE, KINDS * ROWS), 1)
    chosen = ((column >> 5) == (row >> 2)) & ((column & 31) == g * R + (row & 3))
    queries = dot(jnp.where(chosen, 1.0, 0.0).astype(bf16), jnp.concatenate(groups, axis=0)).astype(bf16)

    new = jnp.zeros((2 * 2 * NEW, HD), f32)
    for s in range(peers):
        new = new + received[s, AT_HIGH:MESSAGE].astype(f32)
    new = (new[: 2 * NEW] + new[2 * NEW :]).astype(bf16).astype(f32)
    new_keys = new[:16].astype(bf16)
    new_values = jnp.concatenate([new[NEW : 2 * NEW], jnp.zeros((16 - NEW, HD), f32)], axis=0).astype(bf16)
    row = lax.broadcasted_iota(jnp.int32, (SHARE, 16), 0)
    column = lax.broadcasted_iota(jnp.int32, (SHARE, 16), 1)
    turn = row >> 2
    turn = jnp.where(turn >= ROUNDS, turn - ROUNDS, turn)
    written, place = column >> 2, column & 3
    kept = jnp.where(written == 0, accepted[0, b], jnp.where(written == 1, accepted[1, b], 0))
    visible = ((written < turn) & (place < kept)) | ((written == turn) & (place <= (row & 3)))
    scores = jnp.where(visible, dot_rows(queries, new_keys) * SCALE, NEG)
    new_maxima = jnp.max(scores, axis=1, keepdims=True)
    weights = jnp.where(visible, jnp.exp(scores - new_maxima), 0.0).astype(bf16)
    new_totals = jnp.sum(weights.astype(f32), axis=1, keepdims=True)
    new_sums = dot(weights, new_values)

    stats = received[:, 16:32].astype(f32)[:, AT_STATS - 16 :]
    maxima = stats[:, 0] + (stats[:, 1] + stats[:, 2])
    totals = stats[:, 3] + (stats[:, 4] + stats[:, 5])
    highest = jnp.max(maxima, axis=0, keepdims=True)
    factors = jnp.exp(maxima - highest)
    total = jnp.sum(totals * factors, axis=0, keepdims=True)
    turned = jnp.concatenate(
        [factors, jnp.broadcast_to(highest, (8, 128)), jnp.broadcast_to(total, (8, 128))], axis=0
    ).T[:SHARE]
    sums = jnp.zeros((SHARE, HD), f32)
    for s in range(peers):
        sums = sums + turned[:, s : s + 1] * received[s, :32].astype(f32)[:SHARE]
    highest, total = turned[:, peers : peers + 1], turned[:, peers + 8 : peers + 9]
    overall = jnp.maximum(highest, new_maxima)
    factor, new_factor = jnp.exp(highest - overall), jnp.exp(new_maxima - overall)
    attended = (sums * factor + new_sums * new_factor) / (total * factor + new_totals * new_factor)
    attended = attended.astype(bf16)
    for s in range(peers):
        copies[s] = attended


def projected_kernel(received, w_out, copies):
    rows = received[...].astype(f32)
    share = [
        rows[g * BATCH : (g + 1) * BATCH].reshape(TOKENS, HD).astype(bf16) for g in range(GROUP)
    ]
    out = dot(jnp.concatenate(share, axis=1), w_out[...]).astype(bf16)
    for k in range(copies.shape[0]):
        copies[k] = out


def summed_kernel(received, out):
    total = received[0].astype(f32)
    for k in range(1, received.shape[0]):
        total = total + received[k].astype(f32)
    row = lax.broadcasted_iota(jnp.int32, (TOKENS, TOKENS), 0)
    column = lax.broadcasted_iota(jnp.int32, (TOKENS, TOKENS), 1)
    at = row >> 2
    t, kind, b = at >> 3, (at >> 2) & 1, at & 3
    source = (b * KINDS * ROUNDS + kind * ROUNDS + t) * R + (row & 3)
    order = jnp.where(column == source, 1.0, 0.0).astype(bf16)
    ordered = dot(order, total.astype(bf16)).astype(bf16)
    out[...] = ordered.reshape(out.shape)


def in_vmem(count):
    return [pl.BlockSpec(memory_space=pltpu.VMEM)] * count


def per_device(
    hidden_new,
    w_kv,
    w_out,
    queries_draft,
    queries_verify,
    keys_cache,
    values_cache,
    key_levels,
    value_levels,
    key_scales,
    value_scales,
    lengths,
    accepted,
):
    peers, heads = lax.axis_size("seq"), lax.axis_size("tp")
    params = pltpu.CompilerParams(vmem_limit_bytes=VMEM_LIMIT)
    scales = [x.reshape(BATCH, -1, 128) for x in (key_scales, value_scales)]
    message = partials(
        hidden_new,
        w_kv.reshape(w_kv.shape[0], -1),
        queries_draft,
        queries_verify,
        (keys_cache, values_cache, key_levels, value_levels),
        scales,
        lengths,
    ).reshape(peers, MESSAGE, HD)
    received = lax.all_to_all(message, "seq", 0, 0, tiled=True)
    copies = pl.pallas_call(
        joined_kernel,
        out_shape=jax.ShapeDtypeStruct((peers, SHARE, HD), bf16),
        in_specs=[pl.BlockSpec(memory_space=pltpu.SMEM)] + in_vmem(3),
        out_specs=pl.BlockSpec(memory_space=pltpu.VMEM),
        compiler_params=params,
        name="joined",
    )(accepted, received, queries_draft, queries_verify)
    received = lax.all_to_all(copies, "seq", 0, 0, tiled=True)
    copies = pl.pallas_call(
        projected_kernel,
        out_shape=jax.ShapeDtypeStruct((heads, TOKENS, w_out.shape[1]), bf16),
        in_specs=in_vmem(2),
        out_specs=pl.BlockSpec(memory_space=pltpu.VMEM),
        compiler_params=params,
        name="projected",
    )(received, w_out)
    received = lax.all_to_all(copies, "tp", 0, 0, tiled=True)
    return pl.pallas_call(
        summed_kernel,
        out_shape=jax.ShapeDtypeStruct((ROUNDS, KINDS, BATCH * R, w_out.shape[1]), bf16),
        in_specs=in_vmem(1),
        out_specs=pl.BlockSpec(memory_space=pltpu.VMEM),
        compiler_params=params,
        name="summed",
    )(received)


def solution(mesh):
    in_specs = (
        P(None, None, "seq"),
        P("seq", "tp", None),
        P("tp", "seq"),
        P(None, None, "tp", None, None),
        P(None, None, "tp", None, None),
        P(None, "tp", "seq", None),
        P(None, "tp", "seq", None),
        P(None, "tp", "seq", None),
        P(None, "tp", "seq", None),
        P(None, "tp", "seq"),
        P(None, "tp", "seq"),
        P(),
        P(),
    )
    return jax.shard_map(
        per_device,
        mesh=mesh,
        in_specs=in_specs,
        out_specs=P(None, None, None, "seq"),
        check_vma=False,
    )
```

time: 249 us -> 78.7 us (0.32)
  matrix products: 44.7 us -> 0 us
  other arithmetic: 33.4 us -> 0 us
  waiting for transfers between devices: 31.4 us -> 0 us
  starting transfers between devices: 23.6 us -> 0 us
  blocking collectives: 74 us -> 56.3 us
  local copies, waits for them, and re-layouts: 25.8 us -> 8.79 us
  between operations: 13.8 us -> 0.05 us
  Pallas kernels: 0 us -> 13.1 us
    all_to_all x0 -> x3, blocking collectives: none -> 56.3 us  [the longest x1 25.5 us: per_device(): received = lax.all_to_all(message, 'seq', 0, 0, tiled=True)]
    dot_general x30 -> x0, matrix products: 44.7 us -> none  [the longest x12 27.5 us: attend(): jnp.einsum('bhqd,bhkd->bhqk', queries, keys, preferred_element_type=jnp.f...]
    psum x2 -> x0, blocking collectives: 41.7 us -> none  [one_axis_at_a_time(): shard = lax.psum(shard, axis)]
    all_gather x3 -> x0, blocking collectives: 32.3 us -> none  [all_in_one(): both, at, found = (lax.all_gather(jnp.concatenate(lines), axis), 0, {})]
    all_to_all x3 -> x0, starting transfers between devices: 23.3 us -> none  [sent_to_all(): lax.all_to_all(jnp.broadcast_to(shard[None], (peers, *shard.shape)), axis...]
    all_gather x3 -> x0, waiting for transfers between devices: 16.1 us -> none  [all_in_one(): both, at, found = (lax.all_gather(jnp.concatenate(lines), axis), 0, {})]
    all_to_all x3 -> x0, waiting for transfers between devices: 15.2 us -> none  [sent_to_all(): lax.all_to_all(jnp.broadcast_to(shard[None], (peers, *shard.shape)), axis...]
    add x20 -> x0, other arithmetic: 13.3 us -> none  [the longest x6 8.2 us: combine(): former[2] * former_w[..., None] + latter[2] * latter_w[..., None]]
  transfers between devices with their start and end apart: 6 -> 0, of which waited for: 5 -> 0; matrix products, arithmetic and copies ran while one was open for 27% -> 0% of each run, Pallas kernels for 0% -> 0%
where the time goes in v1:
time: 78.7 us; the launch traced here: 78.2 us
  blocking collectives  56.3 us (72%)
  Pallas kernels  13.1 us (17%)
  local copies, waits for them, and re-layouts  8.79 us (11%)
    all_to_all x1, blocking collectives, per_device(): received = lax.all_to_all(message, 'seq', 0, 0, tiled=True)  25.5 us
    all_to_all x1, blocking collectives, per_device(): received = lax.all_to_all(copies, 'tp', 0, 0, tiled=True)  15.6 us
    all_to_all x1, blocking collectives, per_device(): received = lax.all_to_all(copies, 'seq', 0, 0, tiled=True)  15.2 us
    pallas_call x1, Pallas kernels, partials(): pl.pallas_call(partials_kernel, out_shape=jax.ShapeDtypeStruct((GROUP, BA...  10.9 us
    unnamed x26, local copies, waits for them, and re-layouts  8.79 us

profile of v1, /device:TPU:1, one launch (start us, length us, event | category | flops | bytes accessed | tf_op | source)
XLA Modules:
  0.0 78.2 jit_solution(3030900443719293328)
XLA Ops:
  0.0 0.0 copy-start
  0.0 1.6 %copy-done = bf16[4,1,2048,128]{3,2,1,0:T(8,128)(2,1)S(1)} copy-done((bf16[4,1,2048,128]{3,2,1,0:T(8,128)(2,1)S(1)}, bf16[4,1,2048,128]{3,2,1,0:T(8,128)(2,1)}, u32[]{:S(2)}) %copy-start) | copy-done | bytes 2097176
  1.6 0.0 copy-start.1
  1.6 1.6 %copy-done.1 = bf16[4,1,2048,128]{3,2,1,0:T(8,128)(2,1)S(1)} copy-done((bf16[4,1,2048,128]{3,2,1,0:T(8,128)(2,1)S(1)}, bf16[4,1,2048,128]{3,2,1,0:T(8,128)(2,1)}, u32[]{:S(2)}) %copy-start.1) | copy-done | bytes 2097176
  3.2 0.0 copy-start.3
  3.2 0.9 %copy-done.3 = bf16[3,4,1,32,128]{4,3,2,1,0:T(8,128)(2,1)S(1)} copy-done((bf16[3,4,1,32,128]{4,3,2,1,0:T(8,128)(2,1)S(1)}, bf16[3,4,1,32,128]{4,3,2,1,0:T(8,128)(2,1)}, u32[]{:S(2)}) %copy-start.3) | copy-done | bytes 98328
  4.1 0.9 %copy-done.5 = bf16[3,4,1,32,128]{4,3,2,1,0:T(8,128)(2,1)S(1)} copy-done((bf16[3,4,1,32,128]{4,3,2,1,0:T(8,128)(2,1)S(1)}, bf16[3,4,1,32,128]{4,3,2,1,0:T(8,128)(2,1)}, u32[]{:S(2)}) %copy-start.5) | copy-done | bytes 98328
  5.0 0.9 %copy-done.7 = bf16[256,1,256]{2,0,1:T(8,128)(2,1)S(1)} copy-done((bf16[256,1,256]{2,0,1:T(8,128)(2,1)S(1)}, bf16[256,1,256]{2,0,1:T(8,128)(2,1)}, u32[]{:S(2)}) %copy-start.7) | copy-done | bytes 131096
  5.9 0.8 copy-done.8
  6.6 0.8 copy-done.9
  7.4 0.7 copy-done.10
  8.1 0.7 copy-done.12
  8.8 10.9 %partials.1 = bf16[8,4,80,128]{3,2,1,0:T(8,128)(2,1)S(1)} custom-call(s32[4]{0:T(128)S(1)} %copy-done.12, bf16[3,16,256]{2,1,0:T(8,128)(2,1)S(1)} %copy-done.10, bf16[256,256]{1,0:T(8,128)(2,1)S(1)} %bitcast.5, bf16[3,4,1,32,128]{4,3,2,1,0:T(8,128)(2,1)S(1)} %copy-done.3, bf16[3,4,1,32,128]{4,3,2,1,0:T(8,128)(2,1)S(1)} %copy-done.5, ...), custom_call_target="tpu_custom_call" | custom-call | tf_op jit(solution)/shard_map/partials/pallas_call | solution.py:179
  19.7 0.0 copy-start.2
  19.7 25.5 %all_to_all.15.received = bf16[32,80,128]{2,1,0:T(8,128)(2,1)S(1)} all-to-all(bf16[32,80,128]{2,1,0:T(8,128)(2,1)S(1)} %bitcast.4), channel_id=1, replica_groups=mesh['seq'=32,'tp'=8] {'seq'}, dimensions={0} | all-to-all | bytes 1310720 | tf_op jit(solution)/shard_map/all_to_all | solution.py:307
  45.2 0.0 copy-done.4
  45.2 0.0 copy-done.6
  45.2 0.0 copy-done.11
  45.3 1.2 %joined.1 = bf16[32,24,128]{2,1,0:T(8,128)(2,1)S(1)} custom-call(s32[2,4]{1,0:T(2,128)S(1)} %copy-done.11, bf16[32,80,128]{2,1,0:T(8,128)(2,1)S(1)} %all_to_all.15.received, bf16[3,4,1,32,128]{4,3,2,1,0:T(8,128)(2,1)S(1)} %copy-done.4, bf16[3,4,1,32,128]{4,3,2,1,0:T(8,128)(2,1)S(1)} %copy-done.6), custom_call_target="tpu_custom_call" | custom-call | tf_op jit(solution)/shard_map/joined/pallas_call | solution.py:308
  46.4 15.2 %all_to_all.16.received = bf16[32,24,128]{2,1,0:T(8,128)(2,1)S(1)} all-to-all(bf16[32,24,128]{2,1,0:T(8,128)(2,1)S(1)} %joined.1), channel_id=1, replica_groups=mesh['seq'=32,'tp'=8] {'seq'}, dimensions={0} | all-to-all | bytes 393216 | tf_op jit(solution)/shard_map/all_to_all | solution.py:316
  61.6 0.0 copy-done.2
  61.6 0.2 projected.1
  61.8 15.6 %all_to_all.17.received = bf16[8,96,256]{2,1,0:T(8,128)(2,1)S(1)} all-to-all(bf16[8,96,256]{2,1,0:T(8,128)(2,1)S(1)} %projected.1), channel_id=1, replica_groups=mesh['seq'=32,'tp'=8] {'tp'}, dimensions={0} | all-to-all | bytes 786432 | tf_op jit(solution)/shard_map/all_to_all | solution.py:325
  77.4 0.8 %summed.1 = bf16[3,2,16,256]{3,2,1,0:T(8,128)(2,1)} custom-call(bf16[8,96,256]{2,1,0:T(8,128)(2,1)S(1)} %all_to_all.17.received), custom_call_target="tpu_custom_call" | custom-call | tf_op jit(solution)/shard_map/summed/pallas_call | solution.py:326
  (9 shorter events, 0.0 us)
Async XLA Ops:
  0.0 1.6 %copy-start = (bf16[4,1,2048,128]{3,2,1,0:T(8,128)(2,1)S(1)}, bf16[4,1,2048,128]{3,2,1,0:T(8,128)(2,1)}, u32[]{:S(2)}) copy-start(bf16[4,1,2048,128]{3,2,1,0:T(8,128)(2,1)} %keys.1) | copy-start | bytes 6291460
  1.6 1.6 %copy-start.1 = (bf16[4,1,2048,128]{3,2,1,0:T(8,128)(2,1)S(1)}, bf16[4,1,2048,128]{3,2,1,0:T(8,128)(2,1)}, u32[]{:S(2)}) copy-start(bf16[4,1,2048,128]{3,2,1,0:T(8,128)(2,1)} %values.1) | copy-start | bytes 6291460
  3.2 0.9 %copy-start.3 = (bf16[3,4,1,32,128]{4,3,2,1,0:T(8,128)(2,1)S(1)}, bf16[3,4,1,32,128]{4,3,2,1,0:T(8,128)(2,1)}, u32[]{:S(2)}) copy-start(bf16[3,4,1,32,128]{4,3,2,1,0:T(8,128)(2,1)} %queries_draft.3) | copy-start | bytes 294916
  4.1 0.9 %copy-start.5 = (bf16[3,4,1,32,128]{4,3,2,1,0:T(8,128)(2,1)S(1)}, bf16[3,4,1,32,128]{4,3,2,1,0:T(8,128)(2,1)}, u32[]{:S(2)}) copy-start(bf16[3,4,1,32,128]{4,3,2,1,0:T(8,128)(2,1)} %queries_verify.3) | copy-start | bytes 294916
  5.0 0.9 %copy-start.7 = (bf16[256,1,256]{2,0,1:T(8,128)(2,1)S(1)}, bf16[256,1,256]{2,0,1:T(8,128)(2,1)}, u32[]{:S(2)}) copy-start(bf16[256,1,256]{2,0,1:T(8,128)(2,1)} %param.14) | copy-start | bytes 393220
  5.9 0.8 copy-start.8
  6.6 0.8 copy-start.9
  7.4 0.7 copy-start.10
  8.1 0.7 copy-start.12
  8.8 36.5 %copy-start.4 = (bf16[3,4,1,32,128]{4,3,2,1,0:T(8,128)(2,1)S(1)}, bf16[3,4,1,32,128]{4,3,2,1,0:T(8,128)(2,1)}, u32[]{:S(2)}) copy-start(bf16[3,4,1,32,128]{4,3,2,1,0:T(8,128)(2,1)} %queries_draft.3) | copy-start | bytes 294916
  8.8 36.5 %copy-start.6 = (bf16[3,4,1,32,128]{4,3,2,1,0:T(8,128)(2,1)S(1)}, bf16[3,4,1,32,128]{4,3,2,1,0:T(8,128)(2,1)}, u32[]{:S(2)}) copy-start(bf16[3,4,1,32,128]{4,3,2,1,0:T(8,128)(2,1)} %queries_verify.3) | copy-start | bytes 294916
  8.8 36.5 %copy-start.11 = (s32[2,4]{1,0:T(2,128)S(1)}, s32[2,4]{1,0:T(2,128)}, u32[]{:S(2)}) copy-start(s32[2,4]{1,0:T(2,128)} %accepted.1) | copy-start | bytes 100
  19.7 41.9 %copy-start.2 = (bf16[1024,256]{1,0:T(8,128)(2,1)S(1)}, bf16[1024,256]{1,0:T(8,128)(2,1)}, u32[]{:S(2)}) copy-start(bf16[1024,256]{1,0:T(8,128)(2,1)} %w_out.1) | copy-start | bytes 1572868

commit v2 on v1

--- a/solution.py
+++ b/solution.py
@@ -1,4 +1,3 @@
-import functools
 import math
 
 import jax
@@ -26,6 +25,7 @@
 AT_LOW = AT_HIGH + 2 * NEW
 MESSAGE = AT_LOW + 2 * NEW
 STEP = 512
+FEW = 256
 VMEM_LIMIT = 48 * 1024 * 1024
 
 f32 = jnp.float32
@@ -51,13 +51,12 @@
     return folded
 
 
-def attend(queries, keys, values, usable, scores):
-    positions = scores.shape[1]
+def attend(queries, keys, values, usable, scores, positions):
     step = min(STEP, positions)
     steps = range(0, positions, step)
     highest = None
     for at in steps:
-        part = dot_rows(queries, keys(at, step))
+        part = dot_rows(queries, keys[at : at + step])
         lane = lax.broadcasted_iota(jnp.int32, (1, step), 1) + at
         part = part + jnp.where(lane < usable, 0.0, NEG)
         scores[:, at : at + step] = part
@@ -65,15 +64,27 @@
         highest = folded if highest is None else jnp.maximum(highest, folded)
     highest = jnp.max(highest, axis=1, keepdims=True)
     total = jnp.zeros((queries.shape[0], 128), f32)
-    weighted = jnp.zeros((queries.shape[0], HD), f32)
+    weighted = jnp.zeros((queries.shape[0], KINDS * HD), f32)
     for at in steps:
         weights = jnp.exp2((scores[:, at : at + step] - highest) * SCALE_2).astype(bf16)
         total = total + lanes_folded(weights.astype(f32), jnp.add)
-        weighted = weighted + dot(weights, values(at, step))
+        weighted = weighted + dot(weights, values[at : at + step])
     return highest * SCALE, jnp.sum(total, axis=1, keepdims=True), weighted
 
 
 def partials_kernel(
+    lengths_hbm,
+    hidden_hbm,
+    w_kv_hbm,
+    queries_draft_hbm,
+    queries_verify_hbm,
+    keys_hbm,
+    values_hbm,
+    key_levels_hbm,
+    value_levels_hbm,
+    key_scales_hbm,
+    value_scales_hbm,
+    message,
     lengths,
     hidden,
     w_kv,
@@ -85,118 +96,175 @@
     value_levels,
     key_scales,
     value_scales,
-    message,
     scores,
     sums,
     stats,
     fresh,
     stage,
+    small_sems,
+    cache_sems,
 ):
-    b = pl.program_id(0)
-    local_len = keys.shape[2]
-
-    @pl.when(b == 0)
-    def _():
-        part = dot(hidden[...].reshape(ROUNDS * BATCH * R, hidden.shape[2]), w_kv[...])
-        for k in range(BATCH):
-            for kv in range(2):
-                for t in range(ROUNDS):
-                    fresh[k, kv * NEW + t * R : kv * NEW + (t + 1) * R] = part[
-                        (t * BATCH + k) * R : (t * BATCH + k + 1) * R, kv * HD : (kv + 1) * HD
-                    ]
-
-    usable = jnp.clip(lengths[b] - lax.axis_index("seq") * local_len, 0, local_len)
-    lane = lax.broadcasted_iota(jnp.int32, (ROWS, 128), 1)
-
-    @pl.when(usable == 0)
-    def _():
-        sums[...] = jnp.zeros_like(sums)
-        stats[...] = jnp.where(
-            lax.broadcasted_iota(jnp.int32, stats.shape, 1) == 0, NEG, 0.0
+    local_len = keys.shape[1]
+    few = min(FEW, local_len)
+    small = [
+        pltpu.make_async_copy(source, target, small_sems.at[k])
+        for k, (source, target) in enumerate(
+            (
+                (lengths_hbm, lengths),
+                (queries_draft_hbm, queries_draft),
+                (queries_verify_hbm, queries_verify),
+                (key_scales_hbm, key_scales),
+                (value_scales_hbm, value_scales),
+                (hidden_hbm, hidden),
+                (w_kv_hbm, w_kv),
+            )
         )
-
-    @pl.when(usable > 0)
-    def _():
-        def expanded(levels, scales):
-            columns = scales[0].T
-
-            def rows(at, step):
-                parts = [
-                    (levels[0, 0, k : k + 128].astype(f32) * columns[:, k // 128 : k // 128 + 1]).astype(bf16)
-                    for k in range(at, at + step, 128)
+    ]
+    for copy in small:
+        copy.start()
+    small[0].wait()
+    first = lax.axis_index("seq") * local_len
+
+    def usable_of(b):
+        return jnp.clip(lengths[b] - first, 0, local_len)
+
+    def cache_copies(b, rows):
+        at = pl.ds(0, rows)
+        return [
+            pltpu.make_async_copy(key_levels_hbm.at[b, 0, at], key_levels.at[b, at], cache_sems.at[b, 0]),
+            pltpu.make_async_copy(keys_hbm.at[b, 0, at], keys.at[b, at, pl.ds(HD, HD)], cache_sems.at[b, 1]),
+            pltpu.make_async_copy(value_levels_hbm.at[b, 0, at], value_levels.at[b, at], cache_sems.at[b, 2]),
+            pltpu.make_async_copy(values_hbm.at[b, 0, at], values.at[b, at, pl.ds(HD, HD)], cache_sems.at[b, 3]),
+        ]
+
+    for b in range(BATCH):
+        usable = usable_of(b)
+
+        @pl.when(usable > few)
+        def _():
+            for copy in cache_copies(b, local_len):
+                copy.start()
+
+        @pl.when((usable > 0) & (usable <= few))
+        def _():
+            for copy in cache_copies(b, few):
+                copy.start()
+
+    for copy in small[1:]:
+        copy.wait()
+    part = dot(hidden[...].reshape(ROUNDS * BATCH * R, hidden.shape[2]), w_kv[...])
+    for k in range(BATCH):
+        for kv in range(2):
+            for t in range(ROUNDS):
+                fresh[k, kv * NEW + t * R : kv * NEW + (t + 1) * R] = part[
+                    (t * BATCH + k) * R : (t * BATCH + k + 1) * R, kv * HD : (kv + 1) * HD
                 ]
-                return jnp.concatenate(parts, axis=0)
-
-            return rows
-
-        def plain(cache):
-            return lambda at, step: cache[0, 0, at : at + step]
-
-        draft = (queries_draft, expanded(key_levels, key_scales), expanded(value_levels, value_scales))
-        verify = (queries_verify, plain(keys), plain(values))
-        for kind, (queries, key_rows, value_rows) in enumerate((draft, verify)):
-            rows = queries[...].reshape(ROWS, HD)
-            maxima, totals, weighted = attend(rows, key_rows, value_rows, usable, scores.at[kind])
-            sums[kind * ROWS : (kind + 1) * ROWS] = weighted
-            stats[kind * ROWS : (kind + 1) * ROWS] = jnp.where(lane == 0, maxima, totals)
-
+
+    lane = lax.broadcasted_iota(jnp.int32, (KINDS * ROWS, 128), 1)
     pieces = [
         (g, kt * R, kt * GROUP * R + g * R) for g in range(GROUP) for kt in range(KINDS * ROUNDS)
     ]
-    ordered = []
-    for g, to, at in pieces:
-        stage[g, to : to + R] = sums[at : at + R]
-        ordered.append(stats[at : at + R])
-    turned = jnp.concatenate(
-        [jnp.concatenate(ordered, axis=0), jnp.zeros((256 - KINDS * ROWS, 128), f32)], axis=0
-    ).T
-    maxima, totals = turned[0:1], turned[1:2]
-    parts = []
-    for x in (maxima, totals):
-        high = rounded(x)
-        middle = rounded(x - high)
-        parts += [high, middle, x - high - middle]
-    parts = jnp.concatenate(parts + [jnp.zeros((2, 256), f32)], axis=0)
-    high = rounded(fresh[b])
-    low = fresh[b] - high
-    for g in range(GROUP):
-        stage[g, AT_STATS:AT_HIGH] = jnp.zeros((8, 128), f32)
-        stage[g, AT_STATS:AT_HIGH, :SHARE] = parts[:, g * SHARE : (g + 1) * SHARE]
-        stage[g, AT_HIGH:AT_LOW] = high
-        stage[g, AT_LOW:] = low
-    message[:, 0] = stage[...].astype(bf16)
-
-
-def partials(hidden, w_kv, queries_draft, queries_verify, caches, scales, lengths):
-    local_len = caches[0].shape[2]
-
-    def whole(shape):
-        return pl.BlockSpec(shape, lambda b, lengths: (0,) * len(shape))
-
-    queries = pl.BlockSpec((ROUNDS, 1, 1, GROUP * R, HD), lambda b, lengths: (0, b, 0, 0, 0))
-    cache = pl.BlockSpec((1, 1, local_len, HD), lambda b, lengths: (b, 0, 0, 0))
-    scale = pl.BlockSpec((1, local_len // 128, 128), lambda b, lengths: (b, 0, 0))
+
+    def sequence(b, _):
+        usable = usable_of(b)
+
+        def over(positions):
+            copies = cache_copies(b, positions)
+            for levels, scales, target, ready in (
+                (key_levels, key_scales, keys, copies[:2]),
+                (value_levels, value_scales, values, copies[2:]),
+            ):
+                columns = scales[b].T
+                for copy in ready:
+                    copy.wait()
+                for k in range(positions // 128):
+                    at = pl.ds(k * 128, 128)
+                    low = levels[b, at].astype(f32) * columns[:, k : k + 1]
+                    target[b, at, :HD] = low.astype(bf16)
+            zeros = jnp.zeros((ROWS, HD), bf16)
+            rows = jnp.concatenate(
+                [
+                    jnp.concatenate([queries_draft[:, b, 0].reshape(ROWS, HD), zeros], axis=1),
+                    jnp.concatenate([zeros, queries_verify[:, b, 0].reshape(ROWS, HD)], axis=1),
+                ],
+                axis=0,
+            )
+            maxima, totals, weighted = attend(rows, keys.at[b], values.at[b], usable, scores, positions)
+            sums[:ROWS] = weighted[:ROWS, :HD]
+            sums[ROWS:] = weighted[ROWS:, HD:]
+            stats[...] = jnp.where(lane == 0, maxima, totals)
+
+        @pl.when(usable == 0)
+        def _():
+            sums[...] = jnp.zeros_like(sums)
+            stats[...] = jnp.where(lane == 0, NEG, 0.0)
+
+        @pl.when((usable > 0) & (usable <= few))
+        def _():
+            over(few)
+
+        @pl.when(usable > few)
+        def _():
+            over(local_len)
+
+        ordered = []
+        for g, to, at in pieces:
+            stage[g, to : to + R] = sums[at : at + R]
+            ordered.append(stats[at : at + R])
+        turned = jnp.concatenate(
+            [jnp.concatenate(ordered, axis=0), jnp.zeros((256 - KINDS * ROWS, 128), f32)], axis=0
+        ).T
+        parts = []
+        for x in (turned[0:1], turned[1:2]):
+            high = rounded(x)
+            middle = rounded(x - high)
+            parts += [high, middle, x - high - middle]
+        parts = jnp.concatenate(parts + [jnp.zeros((2, 256), f32)], axis=0)
+        high = rounded(fresh[b])
+        low = fresh[b] - high
+        for g in range(GROUP):
+            stage[g, AT_STATS:AT_HIGH] = jnp.zeros((8, 128), f32)
+            stage[g, AT_STATS:AT_HIGH, :SHARE] = parts[:, g * SHARE : (g + 1) * SHARE]
+            stage[g, AT_HIGH:AT_LOW] = high
+            stage[g, AT_LOW:] = low
+        message[:, b] = stage[...].astype(bf16)
+        return 0
+
+    lax.fori_loop(0, BATCH, sequence, 0)
+
+
+def partials(lengths, *arrays):
+    local_len = arrays[4].shape[2]
+    hidden, w_kv, queries = arrays[:3]
+    blocks = local_len // 128
     return pl.pallas_call(
         partials_kernel,
         out_shape=jax.ShapeDtypeStruct((GROUP, BATCH, MESSAGE, HD), bf16),
-        grid_spec=pltpu.PrefetchScalarGridSpec(
-            num_scalar_prefetch=1,
-            grid=(BATCH,),
-            in_specs=[whole(hidden.shape), whole(w_kv.shape), queries, queries]
-            + [cache] * 4
-            + [scale] * 2,
-            out_specs=pl.BlockSpec((GROUP, 1, MESSAGE, HD), lambda b, lengths: (0, b, 0, 0)),
-            scratch_shapes=[
-                pltpu.VMEM((KINDS, ROWS, local_len), f32),
-                pltpu.VMEM((KINDS * ROWS, HD), f32),
-                pltpu.VMEM((KINDS * ROWS, 128), f32),
-                pltpu.VMEM((BATCH, 2 * NEW, HD), f32),
-                pltpu.VMEM((GROUP, MESSAGE, HD), f32),
-            ],
-        ),
+        in_specs=[pl.BlockSpec(memory_space=pltpu.HBM)] * (1 + len(arrays)),
+        out_specs=pl.BlockSpec(memory_space=pltpu.VMEM),
+        scratch_shapes=[
+            pltpu.SMEM((BATCH,), jnp.int32),
+            pltpu.VMEM(hidden.shape, bf16),
+            pltpu.VMEM(w_kv.shape, bf16),
+            pltpu.VMEM(queries.shape, bf16),
+            pltpu.VMEM(queries.shape, bf16),
+            pltpu.VMEM((BATCH, local_len, KINDS * HD), bf16),
+            pltpu.VMEM((BATCH, local_len, KINDS * HD), bf16),
+            pltpu.VMEM((BATCH, local_len, HD), bf16),
+            pltpu.VMEM((BATCH, local_len, HD), bf16),
+            pltpu.VMEM((BATCH, blocks, 128), f32),
+            pltpu.VMEM((BATCH, blocks, 128), f32),
+            pltpu.VMEM((KINDS * ROWS, local_len), f32),
+            pltpu.VMEM((KINDS * ROWS, HD), f32),
+            pltpu.VMEM((KINDS * ROWS, 128), f32),
+            pltpu.VMEM((BATCH, 2 * NEW, HD), f32),
+            pltpu.VMEM((GROUP, MESSAGE, HD), f32),
+            pltpu.SemaphoreType.DMA((7,)),
+            pltpu.SemaphoreType.DMA((BATCH, 4)),
+        ],
         compiler_params=pltpu.CompilerParams(vmem_limit_bytes=VMEM_LIMIT),
         name="partials",
-    )(lengths, hidden, w_kv, queries_draft, queries_verify, *caches, *scales)
+    )(*(pltpu.with_memory_space_constraint(x, pltpu.HBM) for x in (lengths, *arrays)))
 
 
 def joined_kernel(accepted, received, queries_draft, queries_verify, copies):
@@ -296,13 +364,16 @@
     params = pltpu.CompilerParams(vmem_limit_bytes=VMEM_LIMIT)
     scales = [x.reshape(BATCH, -1, 128) for x in (key_scales, value_scales)]
     message = partials(
+        lengths,
         hidden_new,
         w_kv.reshape(w_kv.shape[0], -1),
         queries_draft,
         queries_verify,
-        (keys_cache, values_cache, key_levels, value_levels),
-        scales,
-        lengths,
+        keys_cache,
+        values_cache,
+        key_levels,
+        value_levels,
+        *scales,
     ).reshape(peers, MESSAGE, HD)
     received = lax.all_to_all(message, "seq", 0, 0, tiled=True)
     copies = pl.pallas_call(

time: 78.7 us -> 68 us (0.86)
  local copies, waits for them, and re-layouts: 8.79 us -> 0.02 us
  Pallas kernels: 13.1 us -> 10.1 us
  blocking collectives: 56.3 us -> 57.7 us
    unnamed x26 -> x8, local copies, waits for them, and re-layouts: 8.79 us -> 0.02 us
    pallas_call x1, Pallas kernels: 10.9 us -> 7.86 us  [partials(): pl.pallas_call(partials_kernel, out_shape=jax.ShapeDtypeStruct((GROUP, BA...]
    all_to_all x1, blocking collectives: 25.5 us -> 26.9 us  [per_device(): received = lax.all_to_all(message, 'seq', 0, 0, tiled=True)]
where the time goes in v2:
time: 68 us; the launch traced here: 67.8 us
  blocking collectives  57.7 us (85%)
  Pallas kernels  10.1 us (15%)
    all_to_all x1, blocking collectives, per_device(): received = lax.all_to_all(message, 'seq', 0, 0, tiled=True)  26.9 us
    all_to_all x1, blocking collectives, per_device(): received = lax.all_to_all(copies, 'tp', 0, 0, tiled=True)  15.6 us
    all_to_all x1, blocking collectives, per_device(): received = lax.all_to_all(copies, 'seq', 0, 0, tiled=True)  15.2 us
    pallas_call x1, Pallas kernels, partials(): pl.pallas_call(partials_kernel, out_shape=jax.ShapeDtypeStruct((GROUP, BA...  7.86 us

profile of v2, /device:TPU:1, one launch (start us, length us, event | category | flops | bytes accessed | tf_op | source)
XLA Modules:
  0.0 67.8 jit_solution(11662988711869166278)
XLA Ops:
  0.0 0.0 copy-start.1
  0.0 0.0 copy-start.2
  0.0 0.0 copy-start.3
  0.0 7.9 %partials.1 = bf16[8,4,80,128]{3,2,1,0:T(8,128)(2,1)S(1)} custom-call(s32[4]{0:T(128)} %lengths_hbm.1, bf16[3,16,256]{2,1,0:T(8,128)(2,1)} %hidden_hbm.1, bf16[256,256]{1,0:T(8,128)(2,1)} %bitcast.5, bf16[3,4,1,32,128]{4,3,2,1,0:T(8,128)(2,1)} %queries_draft.1, bf16[3,4,1,32,128]{4,3,2,1,0:T(8,128)(2,1)} %queries_verify.1, ...), custom_call_target="tpu_custom_call" | custom-call | tf_op jit(solution)/shard_map/partials/pallas_call | solution.py:240
  7.9 0.0 copy-start
  7.9 26.9 %all_to_all.15.received = bf16[32,80,128]{2,1,0:T(8,128)(2,1)S(1)} all-to-all(bf16[32,80,128]{2,1,0:T(8,128)(2,1)S(1)} %bitcast.4), channel_id=1, replica_groups=mesh['seq'=32,'tp'=8] {'seq'}, dimensions={0} | all-to-all | bytes 1310720 | tf_op jit(solution)/shard_map/all_to_all | solution.py:378
  34.8 0.0 copy-done.1
  34.8 0.0 copy-done.2
  34.8 0.0 copy-done.3
  34.8 1.2 %joined.1 = bf16[32,24,128]{2,1,0:T(8,128)(2,1)S(1)} custom-call(s32[2,4]{1,0:T(2,128)S(1)} %copy-done.3, bf16[32,80,128]{2,1,0:T(8,128)(2,1)S(1)} %all_to_all.15.received, bf16[3,4,1,32,128]{4,3,2,1,0:T(8,128)(2,1)S(1)} %copy-done.1, bf16[3,4,1,32,128]{4,3,2,1,0:T(8,128)(2,1)S(1)} %copy-done.2), custom_call_target="tpu_custom_call" | custom-call | tf_op jit(solution)/shard_map/joined/pallas_call | solution.py:379
  36.0 15.2 %all_to_all.16.received = bf16[32,24,128]{2,1,0:T(8,128)(2,1)S(1)} all-to-all(bf16[32,24,128]{2,1,0:T(8,128)(2,1)S(1)} %joined.1), channel_id=1, replica_groups=mesh['seq'=32,'tp'=8] {'seq'}, dimensions={0} | all-to-all | bytes 393216 | tf_op jit(solution)/shard_map/all_to_all | solution.py:387
  51.2 0.0 copy-done
  51.2 0.2 projected.1
  51.4 15.6 %all_to_all.17.received = bf16[8,96,256]{2,1,0:T(8,128)(2,1)S(1)} all-to-all(bf16[8,96,256]{2,1,0:T(8,128)(2,1)S(1)} %projected.1), channel_id=1, replica_groups=mesh['seq'=32,'tp'=8] {'tp'}, dimensions={0} | all-to-all | bytes 786432 | tf_op jit(solution)/shard_map/all_to_all | solution.py:396
  67.0 0.8 %summed.1 = bf16[3,2,16,256]{3,2,1,0:T(8,128)(2,1)} custom-call(bf16[8,96,256]{2,1,0:T(8,128)(2,1)S(1)} %all_to_all.17.received), custom_call_target="tpu_custom_call" | custom-call | tf_op jit(solution)/shard_map/summed/pallas_call | solution.py:397
Async XLA Ops:
  0.0 34.8 %copy-start.1 = (bf16[3,4,1,32,128]{4,3,2,1,0:T(8,128)(2,1)S(1)}, bf16[3,4,1,32,128]{4,3,2,1,0:T(8,128)(2,1)}, u32[]{:S(2)}) copy-start(bf16[3,4,1,32,128]{4,3,2,1,0:T(8,128)(2,1)} %queries_draft.1) | copy-start | bytes 294916
  0.0 34.8 %copy-start.2 = (bf16[3,4,1,32,128]{4,3,2,1,0:T(8,128)(2,1)S(1)}, bf16[3,4,1,32,128]{4,3,2,1,0:T(8,128)(2,1)}, u32[]{:S(2)}) copy-start(bf16[3,4,1,32,128]{4,3,2,1,0:T(8,128)(2,1)} %queries_verify.1) | copy-start | bytes 294916
  0.0 34.8 %copy-start.3 = (s32[2,4]{1,0:T(2,128)S(1)}, s32[2,4]{1,0:T(2,128)}, u32[]{:S(2)}) copy-start(s32[2,4]{1,0:T(2,128)} %accepted.1) | copy-start | bytes 100
  7.9 43.3 %copy-start = (bf16[1024,256]{1,0:T(8,128)(2,1)S(1)}, bf16[1024,256]{1,0:T(8,128)(2,1)}, u32[]{:S(2)}) copy-start(bf16[1024,256]{1,0:T(8,128)(2,1)} %w_out.1) | copy-start | bytes 1572868

commit v3 on v2

--- a/solution.py
+++ b/solution.py
@@ -20,10 +20,9 @@
 SHARE = KINDS * ROUNDS * R
 NEW = ROUNDS * R
 TOKENS = KINDS * ROUNDS * BATCH * R
-AT_STATS = SHARE
-AT_HIGH = SHARE + 8
-AT_LOW = AT_HIGH + 2 * NEW
-MESSAGE = AT_LOW + 2 * NEW
+TAIL = SHARE
+PIECE = 3
+MESSAGE = SHARE + 8
 STEP = 512
 FEW = 256
 VMEM_LIMIT = 48 * 1024 * 1024
@@ -42,6 +41,38 @@
 
 def dot_rows(a, b):
     return lax.dot_general(a, b, (((1,), (1,)), ((), ())), preferred_element_type=f32)
+
+
+def parted(x):
+    high = rounded(x)
+    middle = rounded(x - high)
+    return high, middle, x - high - middle
+
+
+def by_head():
+    row = lax.broadcasted_iota(jnp.int32, (KINDS * ROWS, KINDS * ROWS), 0)
+    column = lax.broadcasted_iota(jnp.int32, (KINDS * ROWS, KINDS * ROWS), 1)
+    target = ((column >> 2) & 7) * SHARE + ((column >> 5) << 2) + (column & 3)
+    return jnp.where(row == target, 1.0, 0.0).astype(bf16)
+
+
+def stats_spread(maxima, totals, place):
+    lane = lax.broadcasted_iota(jnp.int32, (1, 128), 1)
+    part = sum(jnp.where(lane >= k * SHARE, 1, 0) for k in range(1, 5))
+    spread = jnp.zeros((maxima.shape[0], 128), f32)
+    for k, x in enumerate(parted(maxima) + parted(totals)[:2]):
+        spread = jnp.where(part == k, x, spread)
+    return jnp.where(lane - part * SHARE == place, spread, 0.0)
+
+
+def stats_of(rows):
+    turned = rows.T
+    parts = [turned[k * SHARE : (k + 1) * SHARE] for k in range(5)]
+    return parts[0] + (parts[1] + parts[2]), parts[3] + parts[4]
+
+
+def tails_of(received):
+    return received[:, TAIL - 8 :].astype(f32)[:, 8:]
 
 
 def lanes_folded(x, op):
@@ -99,8 +130,8 @@
     scores,
     sums,
     stats,
-    fresh,
-    stage,
+    order,
+    tails,
     small_sems,
     cache_sems,
 ):
@@ -153,17 +184,26 @@
     for copy in small[1:]:
         copy.wait()
     part = dot(hidden[...].reshape(ROUNDS * BATCH * R, hidden.shape[2]), w_kv[...])
-    for k in range(BATCH):
-        for kv in range(2):
-            for t in range(ROUNDS):
-                fresh[k, kv * NEW + t * R : kv * NEW + (t + 1) * R] = part[
-                    (t * BATCH + k) * R : (t * BATCH + k + 1) * R, kv * HD : (kv + 1) * HD
-                ]
-
-    lane = lax.broadcasted_iota(jnp.int32, (KINDS * ROWS, 128), 1)
-    pieces = [
-        (g, kt * R, kt * GROUP * R + g * R) for g in range(GROUP) for kt in range(KINDS * ROUNDS)
-    ]
+    part = jnp.concatenate([part[:, :HD], part[:, HD:]], axis=0)
+    row = lax.broadcasted_iota(jnp.int32, (GROUP * BATCH * 8, 2 * TOKENS // KINDS), 0)
+    column = lax.broadcasted_iota(jnp.int32, (GROUP * BATCH * 8, 2 * TOKENS // KINDS), 1)
+    source = (row >> 3) * PIECE + (row & 7) - 1
+    high = part.astype(bf16)
+    low = (part - high.astype(f32)).astype(bf16)
+    to_high = ((row & 7) >= 1) & ((row & 7) <= PIECE) & (column == source)
+    to_low = ((row & 7) > PIECE) & ((row & 7) <= 2 * PIECE) & (column == source - PIECE)
+    tails[...] = (
+        dot(jnp.where(to_high, 1.0, 0.0).astype(bf16), high)
+        + dot(jnp.where(to_low, 1.0, 0.0).astype(bf16), low)
+    ).reshape(tails.shape)
+    order[...] = by_head()
+
+    row = lax.broadcasted_iota(jnp.int32, (KINDS * ROWS, 1), 0)
+    place = ((row >> 5) << 2) + (row & 3)
+    row = lax.broadcasted_iota(jnp.int32, (GROUP, KINDS * ROWS), 0)
+    column = lax.broadcasted_iota(jnp.int32, (GROUP, KINDS * ROWS), 1)
+    of_head = jnp.where(((column >> 2) & 7) == row, 1.0, 0.0).astype(bf16)
+    first_row = lax.broadcasted_iota(jnp.int32, (GROUP, 8, 128), 1) == 0
 
     def sequence(b, _):
         usable = usable_of(b)
@@ -190,14 +230,15 @@
                 axis=0,
             )
             maxima, totals, weighted = attend(rows, keys.at[b], values.at[b], usable, scores, positions)
-            sums[:ROWS] = weighted[:ROWS, :HD]
-            sums[ROWS:] = weighted[ROWS:, HD:]
-            stats[...] = jnp.where(lane == 0, maxima, totals)
+            sums[:ROWS] = weighted[:ROWS, :HD].astype(bf16)
+            sums[ROWS:] = weighted[ROWS:, HD:].astype(bf16)
+            stats[...] = stats_spread(maxima, totals, place).astype(bf16)
 
         @pl.when(usable == 0)
         def _():
             sums[...] = jnp.zeros_like(sums)
-            stats[...] = jnp.where(lane == 0, NEG, 0.0)
+            none = jnp.zeros((KINDS * ROWS, 1), f32)
+            stats[...] = stats_spread(none + NEG, none, place).astype(bf16)
 
         @pl.when((usable > 0) & (usable <= few))
         def _():
@@ -207,27 +248,10 @@
         def _():
             over(local_len)
 
-        ordered = []
-        for g, to, at in pieces:
-            stage[g, to : to + R] = sums[at : at + R]
-            ordered.append(stats[at : at + R])
-        turned = jnp.concatenate(
-            [jnp.concatenate(ordered, axis=0), jnp.zeros((256 - KINDS * ROWS, 128), f32)], axis=0
-        ).T
-        parts = []
-        for x in (turned[0:1], turned[1:2]):
-            high = rounded(x)
-            middle = rounded(x - high)
-            parts += [high, middle, x - high - middle]
-        parts = jnp.concatenate(parts + [jnp.zeros((2, 256), f32)], axis=0)
-        high = rounded(fresh[b])
-        low = fresh[b] - high
-        for g in range(GROUP):
-            stage[g, AT_STATS:AT_HIGH] = jnp.zeros((8, 128), f32)
-            stage[g, AT_STATS:AT_HIGH, :SHARE] = parts[:, g * SHARE : (g + 1) * SHARE]
-            stage[g, AT_HIGH:AT_LOW] = high
-            stage[g, AT_LOW:] = low
-        message[:, b] = stage[...].astype(bf16)
+        ordered = dot(order[...], sums[...]).reshape(GROUP, SHARE, HD)
+        head_stats = dot(of_head, stats[...]).reshape(GROUP, 1, 128)
+        tail = jnp.where(first_row, head_stats, tails[:, b])
+        message[:, b] = jnp.concatenate([ordered, tail], axis=1).astype(bf16)
         return 0
 
     lax.fori_loop(0, BATCH, sequence, 0)
@@ -255,10 +279,10 @@
             pltpu.VMEM((BATCH, blocks, 128), f32),
             pltpu.VMEM((BATCH, blocks, 128), f32),
             pltpu.VMEM((KINDS * ROWS, local_len), f32),
-            pltpu.VMEM((KINDS * ROWS, HD), f32),
-            pltpu.VMEM((KINDS * ROWS, 128), f32),
-            pltpu.VMEM((BATCH, 2 * NEW, HD), f32),
-            pltpu.VMEM((GROUP, MESSAGE, HD), f32),
+            pltpu.VMEM((KINDS * ROWS, HD), bf16),
+            pltpu.VMEM((KINDS * ROWS, 128), bf16),
+            pltpu.VMEM((KINDS * ROWS, KINDS * ROWS), bf16),
+            pltpu.VMEM((GROUP, BATCH, 8, 128), f32),
             pltpu.SemaphoreType.DMA((7,)),
             pltpu.SemaphoreType.DMA((BATCH, 4)),
         ],
@@ -267,62 +291,75 @@
     )(*(pltpu.with_memory_space_constraint(x, pltpu.HBM) for x in (lengths, *arrays)))
 
 
-def joined_kernel(accepted, received, queries_draft, queries_verify, copies):
+def joined_kernel(received, copies):
     peers = received.shape[0]
-    index = lax.axis_index("seq")
-    g, b = index // BATCH, index % BATCH
-    groups = [q[t, b, 0] for q in (queries_draft, queries_verify) for t in range(ROUNDS)]
-    row = lax.broadcasted_iota(jnp.int32, (SHARE, KINDS * ROWS), 0)
-    column = lax.broadcasted_iota(jnp.int32, (SHARE, KINDS * ROWS), 1)
-    chosen = ((column >> 5) == (row >> 2)) & ((column & 31) == g * R + (row & 3))
-    queries = dot(jnp.where(chosen, 1.0, 0.0).astype(bf16), jnp.concatenate(groups, axis=0)).astype(bf16)
-
-    new = jnp.zeros((2 * 2 * NEW, HD), f32)
-    for s in range(peers):
-        new = new + received[s, AT_HIGH:MESSAGE].astype(f32)
-    new = (new[: 2 * NEW] + new[2 * NEW :]).astype(bf16).astype(f32)
-    new_keys = new[:16].astype(bf16)
-    new_values = jnp.concatenate([new[NEW : 2 * NEW], jnp.zeros((16 - NEW, HD), f32)], axis=0).astype(bf16)
-    row = lax.broadcasted_iota(jnp.int32, (SHARE, 16), 0)
-    column = lax.broadcasted_iota(jnp.int32, (SHARE, 16), 1)
-    turn = row >> 2
-    turn = jnp.where(turn >= ROUNDS, turn - ROUNDS, turn)
-    written, place = column >> 2, column & 3
-    kept = jnp.where(written == 0, accepted[0, b], jnp.where(written == 1, accepted[1, b], 0))
-    visible = ((written < turn) & (place < kept)) | ((written == turn) & (place <= (row & 3)))
-    scores = jnp.where(visible, dot_rows(queries, new_keys) * SCALE, NEG)
-    new_maxima = jnp.max(scores, axis=1, keepdims=True)
-    weights = jnp.where(visible, jnp.exp(scores - new_maxima), 0.0).astype(bf16)
-    new_totals = jnp.sum(weights.astype(f32), axis=1, keepdims=True)
-    new_sums = dot(weights, new_values)
-
-    stats = received[:, 16:32].astype(f32)[:, AT_STATS - 16 :]
-    maxima = stats[:, 0] + (stats[:, 1] + stats[:, 2])
-    totals = stats[:, 3] + (stats[:, 4] + stats[:, 5])
-    highest = jnp.max(maxima, axis=0, keepdims=True)
+    tails = tails_of(received)
+    maxima, totals = stats_of(tails[:, 0])
+    highest = jnp.max(maxima, axis=1, keepdims=True)
     factors = jnp.exp(maxima - highest)
-    total = jnp.sum(totals * factors, axis=0, keepdims=True)
-    turned = jnp.concatenate(
-        [factors, jnp.broadcast_to(highest, (8, 128)), jnp.broadcast_to(total, (8, 128))], axis=0
-    ).T[:SHARE]
+    total = jnp.sum(totals * factors, axis=1, keepdims=True)
     sums = jnp.zeros((SHARE, HD), f32)
     for s in range(peers):
-        sums = sums + turned[:, s : s + 1] * received[s, :32].astype(f32)[:SHARE]
-    highest, total = turned[:, peers : peers + 1], turned[:, peers + 8 : peers + 9]
-    overall = jnp.maximum(highest, new_maxima)
-    factor, new_factor = jnp.exp(highest - overall), jnp.exp(new_maxima - overall)
-    attended = (sums * factor + new_sums * new_factor) / (total * factor + new_totals * new_factor)
-    attended = attended.astype(bf16)
+        sums = sums + factors[:, s : s + 1] * received[s].astype(f32)[:SHARE]
+    fresh = jnp.sum(tails, axis=0)
+    fresh = fresh + jnp.concatenate([fresh[PIECE:], fresh[:PIECE]], axis=0)
+    place = lax.broadcasted_iota(jnp.int32, (SHARE, 1), 0)
+    stats = jnp.sum(stats_spread(highest, total, place), axis=0, keepdims=True)
+    row = lax.broadcasted_iota(jnp.int32, (8, 128), 0)
+    tail = jnp.where(row == 0, stats, jnp.where(row <= PIECE, fresh, 0.0))
+    block = jnp.concatenate([sums / total, tail], axis=0).astype(bf16)
     for s in range(peers):
-        copies[s] = attended
-
-
-def projected_kernel(received, w_out, copies):
-    rows = received[...].astype(f32)
-    share = [
-        rows[g * BATCH : (g + 1) * BATCH].reshape(TOKENS, HD).astype(bf16) for g in range(GROUP)
-    ]
-    out = dot(jnp.concatenate(share, axis=1), w_out[...]).astype(bf16)
+        copies[s] = block
+
+
+def projected_kernel(accepted, received, queries_draft, queries_verify, w_out, copies):
+    peers = received.shape[0]
+    tails = tails_of(received)
+    row = lax.broadcasted_iota(jnp.int32, (BATCH * 2 * 16, peers * 8), 0)
+    column = lax.broadcasted_iota(jnp.int32, (BATCH * 2 * 16, peers * 8), 1)
+    within = (column & 7) - 1
+    source = (column >> 3) * PIECE + within
+    kv = jnp.where(source >= TOKENS // KINDS, 1, 0)
+    token = source - kv * (TOKENS // KINDS)
+    target = ((token >> 2) & 3) * 32 + kv * 16 + ((token >> 4) << 2) + (token & 3)
+    chosen = (within >= 0) & (within < PIECE) & (row == target)
+    fresh = dot(
+        jnp.where(chosen, 1.0, 0.0).astype(bf16), tails.reshape(peers * 8, 128).astype(bf16)
+    ).astype(bf16)
+
+    maxima, totals = stats_of(tails[:, 0])
+    order = by_head()
+    row = lax.broadcasted_iota(jnp.int32, (KINDS * ROWS, 16), 0)
+    column = lax.broadcasted_iota(jnp.int32, (KINDS * ROWS, 16), 1)
+    turn = (row - ((row * 171) >> 12) * SHARE) >> 2
+    turn = jnp.where(turn >= ROUNDS, turn - ROUNDS, turn)
+    written, token = column >> 2, column & 3
+    itself = (written == turn) & (token <= (row & 3))
+    earlier = written < turn
+    parts = []
+    for b in range(BATCH):
+        groups = [q[t, b, 0] for q in (queries_draft, queries_verify) for t in range(ROUNDS)]
+        queries = dot(order, jnp.concatenate(groups, axis=0)).astype(bf16)
+        kept = jnp.where(written == 0, accepted[0, b], jnp.where(written == 1, accepted[1, b], 0))
+        visible = itself | (earlier & (token < kept))
+        scores = jnp.where(visible, dot_rows(queries, fresh[b * 32 : b * 32 + 16]) * SCALE, NEG)
+        new_highest = jnp.max(scores, axis=1, keepdims=True)
+        weights = jnp.where(visible, jnp.exp(scores - new_highest), 0.0).astype(bf16)
+        new_total = jnp.sum(weights.astype(f32), axis=1, keepdims=True)
+        new_sums = dot(weights, fresh[b * 32 + 16 : b * 32 + 32])
+        of_b = range(b, peers, BATCH)
+        highest = jnp.concatenate([maxima[:, p : p + 1] for p in of_b], axis=0)
+        total = jnp.concatenate([totals[:, p : p + 1] for p in of_b], axis=0)
+        means = jnp.concatenate([received[p].astype(f32)[:SHARE] for p in of_b], axis=0)
+        overall = jnp.maximum(highest, new_highest)
+        factor = total * jnp.exp(highest - overall)
+        new_factor = jnp.exp(new_highest - overall)
+        whole = factor + new_total * new_factor
+        attended = means * (factor / whole) + new_sums * (new_factor / whole)
+        parts.append(
+            jnp.concatenate([attended[g * SHARE : (g + 1) * SHARE] for g in range(GROUP)], axis=1)
+        )
+    out = dot(jnp.concatenate(parts, axis=0).astype(bf16), w_out[...]).astype(bf16)
     for k in range(copies.shape[0]):
         copies[k] = out
 
@@ -378,21 +415,21 @@
     received = lax.all_to_all(message, "seq", 0, 0, tiled=True)
     copies = pl.pallas_call(
         joined_kernel,
-        out_shape=jax.ShapeDtypeStruct((peers, SHARE, HD), bf16),
-        in_specs=[pl.BlockSpec(memory_space=pltpu.SMEM)] + in_vmem(3),
+        out_shape=jax.ShapeDtypeStruct((peers, MESSAGE, HD), bf16),
+        in_specs=in_vmem(1),
         out_specs=pl.BlockSpec(memory_space=pltpu.VMEM),
         compiler_params=params,
         name="joined",
-    )(accepted, received, queries_draft, queries_verify)
+    )(received)
     received = lax.all_to_all(copies, "seq", 0, 0, tiled=True)
     copies = pl.pallas_call(
         projected_kernel,
         out_shape=jax.ShapeDtypeStruct((heads, TOKENS, w_out.shape[1]), bf16),
-        in_specs=in_vmem(2),
+        in_specs=[pl.BlockSpec(memory_space=pltpu.SMEM)] + in_vmem(4),
         out_specs=pl.BlockSpec(memory_space=pltpu.VMEM),
         compiler_params=params,
         name="projected",
-    )(received, w_out)
+    )(accepted, received, queries_draft, queries_verify, w_out)
     received = lax.all_to_all(copies, "tp", 0, 0, tiled=True)
     return pl.pallas_call(
         summed_kernel,

time: 68 us -> 62.6 us (0.921)
  blocking collectives: 57.7 us -> 50.6 us
  Pallas kernels: 10.1 us -> 12 us
    all_to_all x1, blocking collectives: 26.9 us -> 19.5 us  [per_device(): received = lax.all_to_all(message, 'seq', 0, 0, tiled=True)]
    pallas_call x1, Pallas kernels: 0.23 us -> 2.37 us  [per_device(): pl.pallas_call(projected_kernel, out_shape=jax.ShapeDtypeStruct((heads, T...]
where the time goes in v3:
time: 62.6 us
  blocking collectives  50.6 us (81%)
  Pallas kernels  12 us (19%)
    all_to_all x1, blocking collectives, per_device(): received = lax.all_to_all(message, 'seq', 0, 0, tiled=True)  19.5 us
    all_to_all x1, blocking collectives, per_device(): received = lax.all_to_all(copies, 'tp', 0, 0, tiled=True)  16.1 us
    all_to_all x1, blocking collectives, per_device(): received = lax.all_to_all(copies, 'seq', 0, 0, tiled=True)  15 us
    pallas_call x1, Pallas kernels, partials(): pl.pallas_call(partials_kernel, out_shape=jax.ShapeDtypeStruct((GROUP, BA...  8.27 us
    pallas_call x1, Pallas kernels, per_device(): pl.pallas_call(projected_kernel, out_shape=jax.ShapeDtypeStruct((heads, T...  2.37 us

profile of v3, /device:TPU:1, one launch (start us, length us, event | category | flops | bytes accessed | tf_op | source)
XLA Modules:
  0.0 62.6 jit_solution(1513349482143359317)
XLA Ops:
  0.0 0.0 copy-start
  0.0 0.0 copy-start.1
  0.0 0.0 copy-start.2
  0.0 0.0 copy-start.3
  0.0 8.3 %partials.1 = bf16[8,4,32,128]{3,2,1,0:T(8,128)(2,1)S(1)} custom-call(s32[4]{0:T(128)} %lengths_hbm.1, bf16[3,16,256]{2,1,0:T(8,128)(2,1)} %hidden_hbm.1, bf16[256,256]{1,0:T(8,128)(2,1)} %bitcast.5, bf16[3,4,1,32,128]{4,3,2,1,0:T(8,128)(2,1)} %queries_draft.1, bf16[3,4,1,32,128]{4,3,2,1,0:T(8,128)(2,1)} %queries_verify.1, ...), custom_call_target="tpu_custom_call" | custom-call | tf_op jit(solution)/shard_map/partials/pallas_call | solution.py:264
  8.3 19.5 %all_to_all.15.received = bf16[32,32,128]{2,1,0:T(8,128)(2,1)S(1)} all-to-all(bf16[32,32,128]{2,1,0:T(8,128)(2,1)S(1)} %bitcast.4), channel_id=1, replica_groups=mesh['seq'=32,'tp'=8] {'seq'}, dimensions={0} | all-to-all | bytes 524288 | tf_op jit(solution)/shard_map/all_to_all | solution.py:415
  27.8 0.5 joined.1
  28.3 15.0 %all_to_all.16.received = bf16[32,32,128]{2,1,0:T(8,128)(2,1)S(1)} all-to-all(bf16[32,32,128]{2,1,0:T(8,128)(2,1)S(1)} %joined.1), channel_id=1, replica_groups=mesh['seq'=32,'tp'=8] {'seq'}, dimensions={0} | all-to-all | bytes 524288 | tf_op jit(solution)/shard_map/all_to_all | solution.py:424
  43.3 0.0 copy-done
  43.3 0.0 copy-done.1
  43.3 0.0 copy-done.2
  43.3 0.0 copy-done.3
  43.3 2.4 %projected.1 = bf16[8,96,256]{2,1,0:T(8,128)(2,1)S(1)} custom-call(s32[2,4]{1,0:T(2,128)S(1)} %copy-done.3, bf16[32,32,128]{2,1,0:T(8,128)(2,1)S(1)} %all_to_all.16.received, bf16[3,4,1,32,128]{4,3,2,1,0:T(8,128)(2,1)S(1)} %copy-done.1, bf16[3,4,1,32,128]{4,3,2,1,0:T(8,128)(2,1)S(1)} %copy-done.2, bf16[1024,256]{1,0:T(8,128)(2,1)S(1)} %copy-done), custom_call_target="tpu_custom_call" | custom-call | tf_op jit(solution)/shard_map/projected/pallas_call | solution.py:425
  45.7 16.1 %all_to_all.17.received = bf16[8,96,256]{2,1,0:T(8,128)(2,1)S(1)} all-to-all(bf16[8,96,256]{2,1,0:T(8,128)(2,1)S(1)} %projected.1), channel_id=1, replica_groups=mesh['seq'=32,'tp'=8] {'tp'}, dimensions={0} | all-to-all | bytes 786432 | tf_op jit(solution)/shard_map/all_to_all | solution.py:433
  61.8 0.8 %summed.1 = bf16[3,2,16,256]{3,2,1,0:T(8,128)(2,1)} custom-call(bf16[8,96,256]{2,1,0:T(8,128)(2,1)S(1)} %all_to_all.17.received), custom_call_target="tpu_custom_call" | custom-call | tf_op jit(solution)/shard_map/summed/pallas_call | solution.py:434
Async XLA Ops:
  0.0 43.3 %copy-start = (bf16[1024,256]{1,0:T(8,128)(2,1)S(1)}, bf16[1024,256]{1,0:T(8,128)(2,1)}, u32[]{:S(2)}) copy-start(bf16[1024,256]{1,0:T(8,128)(2,1)} %w_out.1) | copy-start | bytes 1572868
  0.0 43.3 %copy-start.1 = (bf16[3,4,1,32,128]{4,3,2,1,0:T(8,128)(2,1)S(1)}, bf16[3,4,1,32,128]{4,3,2,1,0:T(8,128)(2,1)}, u32[]{:S(2)}) copy-start(bf16[3,4,1,32,128]{4,3,2,1,0:T(8,128)(2,1)} %queries_draft.1) | copy-start | bytes 294916
  0.0 43.3 %copy-start.2 = (bf16[3,4,1,32,128]{4,3,2,1,0:T(8,128)(2,1)S(1)}, bf16[3,4,1,32,128]{4,3,2,1,0:T(8,128)(2,1)}, u32[]{:S(2)}) copy-start(bf16[3,4,1,32,128]{4,3,2,1,0:T(8,128)(2,1)} %queries_verify.1) | copy-start | bytes 294916
  0.0 43.3 %copy-start.3 = (s32[2,4]{1,0:T(2,128)S(1)}, s32[2,4]{1,0:T(2,128)}, u32[]{:S(2)}) copy-start(s32[2,4]{1,0:T(2,128)} %accepted.1) | copy-start | bytes 100

commit v4 on v3

--- a/solution.py
+++ b/solution.py
@@ -87,9 +87,10 @@
     steps = range(0, positions, step)
     highest = None
     for at in steps:
-        part = dot_rows(queries, keys[at : at + step])
-        lane = lax.broadcasted_iota(jnp.int32, (1, step), 1) + at
-        part = part + jnp.where(lane < usable, 0.0, NEG)
+        part = dot_rows(queries, keys(at, step))
+        if usable is not None:
+            lane = lax.broadcasted_iota(jnp.int32, (1, step), 1) + at
+            part = part + jnp.where(lane < usable, 0.0, NEG)
         scores[:, at : at + step] = part
         folded = lanes_folded(part, jnp.maximum)
         highest = folded if highest is None else jnp.maximum(highest, folded)
@@ -99,7 +100,7 @@
     for at in steps:
         weights = jnp.exp2((scores[:, at : at + step] - highest) * SCALE_2).astype(bf16)
         total = total + lanes_folded(weights.astype(f32), jnp.add)
-        weighted = weighted + dot(weights, values[at : at + step])
+        weighted = weighted + dot(weights, values(at, step))
     return highest * SCALE, jnp.sum(total, axis=1, keepdims=True), weighted
 
 
@@ -162,10 +163,15 @@
     def cache_copies(b, rows):
         at = pl.ds(0, rows)
         return [
-            pltpu.make_async_copy(key_levels_hbm.at[b, 0, at], key_levels.at[b, at], cache_sems.at[b, 0]),
-            pltpu.make_async_copy(keys_hbm.at[b, 0, at], keys.at[b, at, pl.ds(HD, HD)], cache_sems.at[b, 1]),
-            pltpu.make_async_copy(value_levels_hbm.at[b, 0, at], value_levels.at[b, at], cache_sems.at[b, 2]),
-            pltpu.make_async_copy(values_hbm.at[b, 0, at], values.at[b, at, pl.ds(HD, HD)], cache_sems.at[b, 3]),
+            pltpu.make_async_copy(source.at[b, 0, at], target.at[b, at], cache_sems.at[b, k])
+            for k, (source, target) in enumerate(
+                (
+                    (key_levels_hbm, key_levels),
+                    (keys_hbm, keys),
+                    (value_levels_hbm, value_levels),
+                    (values_hbm, values),
+                )
+            )
         ]
 
     for b in range(BATCH):
@@ -181,6 +187,7 @@
             for copy in cache_copies(b, few):
                 copy.start()
 
+    order[...] = by_head()
     for copy in small[1:]:
         copy.wait()
     part = dot(hidden[...].reshape(ROUNDS * BATCH * R, hidden.shape[2]), w_kv[...])
@@ -196,7 +203,6 @@
         dot(jnp.where(to_high, 1.0, 0.0).astype(bf16), high)
         + dot(jnp.where(to_low, 1.0, 0.0).astype(bf16), low)
     ).reshape(tails.shape)
-    order[...] = by_head()
 
     row = lax.broadcasted_iota(jnp.int32, (KINDS * ROWS, 1), 0)
     place = ((row >> 5) << 2) + (row & 3)
@@ -208,19 +214,24 @@
     def sequence(b, _):
         usable = usable_of(b)
 
-        def over(positions):
+        def over(positions, masked):
             copies = cache_copies(b, positions)
-            for levels, scales, target, ready in (
-                (key_levels, key_scales, keys, copies[:2]),
-                (value_levels, value_scales, values, copies[2:]),
-            ):
+
+            def both(levels, scales, plain, ready):
                 columns = scales[b].T
-                for copy in ready:
-                    copy.wait()
-                for k in range(positions // 128):
-                    at = pl.ds(k * 128, 128)
-                    low = levels[b, at].astype(f32) * columns[:, k : k + 1]
-                    target[b, at, :HD] = low.astype(bf16)
+
+                def rows(at, step):
+                    if at == 0:
+                        for copy in ready:
+                            copy.wait()
+                    low = [
+                        (levels[b, k : k + 128].astype(f32) * columns[:, k // 128 : k // 128 + 1]).astype(bf16)
+                        for k in range(at, at + step, 128)
+                    ]
+                    return jnp.concatenate([jnp.concatenate(low, axis=0), plain[b, at : at + step]], axis=1)
+
+                return rows
+
             zeros = jnp.zeros((ROWS, HD), bf16)
             rows = jnp.concatenate(
                 [
@@ -229,32 +240,44 @@
                 ],
                 axis=0,
             )
-            maxima, totals, weighted = attend(rows, keys.at[b], values.at[b], usable, scores, positions)
-            sums[:ROWS] = weighted[:ROWS, :HD].astype(bf16)
-            sums[ROWS:] = weighted[ROWS:, HD:].astype(bf16)
-            stats[...] = stats_spread(maxima, totals, place).astype(bf16)
+            maxima, totals, weighted = attend(
+                rows,
+                both(key_levels, key_scales, keys, copies[:2]),
+                both(value_levels, value_scales, values, copies[2:]),
+                usable if masked else None,
+                scores,
+                positions,
+            )
+            sums[b, :ROWS] = weighted[:ROWS, :HD].astype(bf16)
+            sums[b, ROWS:] = weighted[ROWS:, HD:].astype(bf16)
+            stats[b] = stats_spread(maxima, totals, place).astype(bf16)
 
         @pl.when(usable == 0)
         def _():
-            sums[...] = jnp.zeros_like(sums)
+            sums[b] = jnp.zeros((KINDS * ROWS, HD), bf16)
             none = jnp.zeros((KINDS * ROWS, 1), f32)
-            stats[...] = stats_spread(none + NEG, none, place).astype(bf16)
+            stats[b] = stats_spread(none + NEG, none, place).astype(bf16)
 
         @pl.when((usable > 0) & (usable <= few))
         def _():
-            over(few)
-
-        @pl.when(usable > few)
-        def _():
-            over(local_len)
-
-        ordered = dot(order[...], sums[...]).reshape(GROUP, SHARE, HD)
-        head_stats = dot(of_head, stats[...]).reshape(GROUP, 1, 128)
+            over(few, True)
+
+        @pl.when((usable > few) & (usable < local_len))
+        def _():
+            over(local_len, True)
+
+        @pl.when(usable == local_len)
+        def _():
+            over(local_len, False)
+
+        return 0
+
+    lax.fori_loop(0, BATCH, sequence, 0)
+    for b in range(BATCH):
+        ordered = dot(order[...], sums[b]).reshape(GROUP, SHARE, HD)
+        head_stats = dot(of_head, stats[b]).reshape(GROUP, 1, 128)
         tail = jnp.where(first_row, head_stats, tails[:, b])
         message[:, b] = jnp.concatenate([ordered, tail], axis=1).astype(bf16)
-        return 0
-
-    lax.fori_loop(0, BATCH, sequence, 0)
 
 
 def partials(lengths, *arrays):
@@ -272,15 +295,15 @@
             pltpu.VMEM(w_kv.shape, bf16),
             pltpu.VMEM(queries.shape, bf16),
             pltpu.VMEM(queries.shape, bf16),
-            pltpu.VMEM((BATCH, local_len, KINDS * HD), bf16),
-            pltpu.VMEM((BATCH, local_len, KINDS * HD), bf16),
+            pltpu.VMEM((BATCH, local_len, HD), bf16),
+            pltpu.VMEM((BATCH, local_len, HD), bf16),
             pltpu.VMEM((BATCH, local_len, HD), bf16),
             pltpu.VMEM((BATCH, local_len, HD), bf16),
             pltpu.VMEM((BATCH, blocks, 128), f32),
             pltpu.VMEM((BATCH, blocks, 128), f32),
             pltpu.VMEM((KINDS * ROWS, local_len), f32),
-            pltpu.VMEM((KINDS * ROWS, HD), bf16),
-            pltpu.VMEM((KINDS * ROWS, 128), bf16),
+            pltpu.VMEM((BATCH, KINDS * ROWS, HD), bf16),
+            pltpu.VMEM((BATCH, KINDS * ROWS, 128), bf16),
             pltpu.VMEM((KINDS * ROWS, KINDS * ROWS), bf16),
             pltpu.VMEM((GROUP, BATCH, 8, 128), f32),
             pltpu.SemaphoreType.DMA((7,)),

time: 62.6 us -> 62 us (level)
  Pallas kernels: 12 us -> 11 us
    pallas_call x1, Pallas kernels: 8.27 us -> 7.28 us  [partials(): pl.pallas_call(partials_kernel, out_shape=jax.ShapeDtypeStruct((GROUP, BA...]
where the time goes in v4:
time: 62 us; the launch traced here: 61.8 us
  blocking collectives  50.8 us (82%)
  Pallas kernels  11 us (18%)
    all_to_all x1, blocking collectives, per_device(): received = lax.all_to_all(message, 'seq', 0, 0, tiled=True)  19.7 us
    all_to_all x1, blocking collectives, per_device(): received = lax.all_to_all(copies, 'tp', 0, 0, tiled=True)  16.1 us
    all_to_all x1, blocking collectives, per_device(): received = lax.all_to_all(copies, 'seq', 0, 0, tiled=True)  15 us
    pallas_call x1, Pallas kernels, partials(): pl.pallas_call(partials_kernel, out_shape=jax.ShapeDtypeStruct((GROUP, BA...  7.28 us
    pallas_call x1, Pallas kernels, per_device(): pl.pallas_call(projected_kernel, out_shape=jax.ShapeDtypeStruct((heads, T...  2.36 us

profile of v4, /device:TPU:1, one launch (start us, length us, event | category | flops | bytes accessed | tf_op | source)
XLA Modules:
  0.0 61.8 jit_solution(7601936395526262708)
XLA Ops:
  0.0 0.0 copy-start
  0.0 0.0 copy-start.1
  0.0 0.0 copy-start.2
  0.0 0.0 copy-start.3
  0.0 7.3 %partials.1 = bf16[8,4,32,128]{3,2,1,0:T(8,128)(2,1)S(1)} custom-call(s32[4]{0:T(128)} %lengths_hbm.1, bf16[3,16,256]{2,1,0:T(8,128)(2,1)} %hidden_hbm.1, bf16[256,256]{1,0:T(8,128)(2,1)} %bitcast.5, bf16[3,4,1,32,128]{4,3,2,1,0:T(8,128)(2,1)} %queries_draft.1, bf16[3,4,1,32,128]{4,3,2,1,0:T(8,128)(2,1)} %queries_verify.1, ...), custom_call_target="tpu_custom_call" | custom-call | tf_op jit(solution)/shard_map/partials/pallas_call | solution.py:287
  7.3 19.7 %all_to_all.15.received = bf16[32,32,128]{2,1,0:T(8,128)(2,1)S(1)} all-to-all(bf16[32,32,128]{2,1,0:T(8,128)(2,1)S(1)} %bitcast.4), channel_id=1, replica_groups=mesh['seq'=32,'tp'=8] {'seq'}, dimensions={0} | all-to-all | bytes 524288 | tf_op jit(solution)/shard_map/all_to_all | solution.py:438
  27.0 0.5 joined.1
  27.5 15.0 %all_to_all.16.received = bf16[32,32,128]{2,1,0:T(8,128)(2,1)S(1)} all-to-all(bf16[32,32,128]{2,1,0:T(8,128)(2,1)S(1)} %joined.1), channel_id=1, replica_groups=mesh['seq'=32,'tp'=8] {'seq'}, dimensions={0} | all-to-all | bytes 524288 | tf_op jit(solution)/shard_map/all_to_all | solution.py:447
  42.5 0.0 copy-done
  42.5 0.0 copy-done.1
  42.5 0.0 copy-done.2
  42.5 0.0 copy-done.3
  42.5 2.4 %projected.1 = bf16[8,96,256]{2,1,0:T(8,128)(2,1)S(1)} custom-call(s32[2,4]{1,0:T(2,128)S(1)} %copy-done.3, bf16[32,32,128]{2,1,0:T(8,128)(2,1)S(1)} %all_to_all.16.received, bf16[3,4,1,32,128]{4,3,2,1,0:T(8,128)(2,1)S(1)} %copy-done.1, bf16[3,4,1,32,128]{4,3,2,1,0:T(8,128)(2,1)S(1)} %copy-done.2, bf16[1024,256]{1,0:T(8,128)(2,1)S(1)} %copy-done), custom_call_target="tpu_custom_call" | custom-call | tf_op jit(solution)/shard_map/projected/pallas_call | solution.py:448
  44.9 16.1 %all_to_all.17.received = bf16[8,96,256]{2,1,0:T(8,128)(2,1)S(1)} all-to-all(bf16[8,96,256]{2,1,0:T(8,128)(2,1)S(1)} %projected.1), channel_id=1, replica_groups=mesh['seq'=32,'tp'=8] {'tp'}, dimensions={0} | all-to-all | bytes 786432 | tf_op jit(solution)/shard_map/all_to_all | solution.py:456
  61.0 0.8 %summed.1 = bf16[3,2,16,256]{3,2,1,0:T(8,128)(2,1)} custom-call(bf16[8,96,256]{2,1,0:T(8,128)(2,1)S(1)} %all_to_all.17.received), custom_call_target="tpu_custom_call" | custom-call | tf_op jit(solution)/shard_map/summed/pallas_call | solution.py:457
Async XLA Ops:
  0.0 42.5 %copy-start = (bf16[1024,256]{1,0:T(8,128)(2,1)S(1)}, bf16[1024,256]{1,0:T(8,128)(2,1)}, u32[]{:S(2)}) copy-start(bf16[1024,256]{1,0:T(8,128)(2,1)} %w_out.1) | copy-start | bytes 1572868
  0.0 42.5 %copy-start.1 = (bf16[3,4,1,32,128]{4,3,2,1,0:T(8,128)(2,1)S(1)}, bf16[3,4,1,32,128]{4,3,2,1,0:T(8,128)(2,1)}, u32[]{:S(2)}) copy-start(bf16[3,4,1,32,128]{4,3,2,1,0:T(8,128)(2,1)} %queries_draft.1) | copy-start | bytes 294916
  0.0 42.5 %copy-start.2 = (bf16[3,4,1,32,128]{4,3,2,1,0:T(8,128)(2,1)S(1)}, bf16[3,4,1,32,128]{4,3,2,1,0:T(8,128)(2,1)}, u32[]{:S(2)}) copy-start(bf16[3,4,1,32,128]{4,3,2,1,0:T(8,128)(2,1)} %queries_verify.1) | copy-start | bytes 294916
  0.0 42.5 %copy-start.3 = (s32[2,4]{1,0:T(2,128)S(1)}, s32[2,4]{1,0:T(2,128)}, u32[]{:S(2)}) copy-start(s32[2,4]{1,0:T(2,128)} %accepted.1) | copy-start | bytes 100

commit v5 on v4

--- a/solution.py
+++ b/solution.py
@@ -335,22 +335,7 @@
         copies[s] = block
 
 
-def projected_kernel(accepted, received, queries_draft, queries_verify, w_out, copies):
-    peers = received.shape[0]
-    tails = tails_of(received)
-    row = lax.broadcasted_iota(jnp.int32, (BATCH * 2 * 16, peers * 8), 0)
-    column = lax.broadcasted_iota(jnp.int32, (BATCH * 2 * 16, peers * 8), 1)
-    within = (column & 7) - 1
-    source = (column >> 3) * PIECE + within
-    kv = jnp.where(source >= TOKENS // KINDS, 1, 0)
-    token = source - kv * (TOKENS // KINDS)
-    target = ((token >> 2) & 3) * 32 + kv * 16 + ((token >> 4) << 2) + (token & 3)
-    chosen = (within >= 0) & (within < PIECE) & (row == target)
-    fresh = dot(
-        jnp.where(chosen, 1.0, 0.0).astype(bf16), tails.reshape(peers * 8, 128).astype(bf16)
-    ).astype(bf16)
-
-    maxima, totals = stats_of(tails[:, 0])
+def prepared_kernel(_, accepted, queries_draft, queries_verify, queries, hidden, chosen, gather):
     order = by_head()
     row = lax.broadcasted_iota(jnp.int32, (KINDS * ROWS, 16), 0)
     column = lax.broadcasted_iota(jnp.int32, (KINDS * ROWS, 16), 1)
@@ -359,15 +344,40 @@
     written, token = column >> 2, column & 3
     itself = (written == turn) & (token <= (row & 3))
     earlier = written < turn
+    for b in range(BATCH):
+        groups = [q[t, b, 0] for q in (queries_draft, queries_verify) for t in range(ROUNDS)]
+        queries[b] = dot(order, jnp.concatenate(groups, axis=0)).astype(bf16)
+        kept = jnp.where(written == 0, accepted[0, b], jnp.where(written == 1, accepted[1, b], 0))
+        hidden[b] = jnp.where(itself | (earlier & (token < kept)), 0.0, NEG)
+    row = lax.broadcasted_iota(jnp.int32, chosen.shape, 0)
+    column = lax.broadcasted_iota(jnp.int32, chosen.shape, 1)
+    within = (column & 7) - 1
+    source = (column >> 3) * PIECE + within
+    kv = jnp.where(source >= TOKENS // KINDS, 1, 0)
+    token = source - kv * (TOKENS // KINDS)
+    target = ((token >> 2) & 3) * 32 + kv * 16 + ((token >> 4) << 2) + (token & 3)
+    taken = (within >= 0) & (within < PIECE) & (row == target)
+    chosen[...] = jnp.where(taken, 1.0, 0.0).astype(bf16)
+    row = lax.broadcasted_iota(jnp.int32, gather.shape, 0)
+    column = lax.broadcasted_iota(jnp.int32, gather.shape, 1)
+    at = row >> 2
+    t, kind, b = at >> 3, (at >> 2) & 1, at & 3
+    source = (b * KINDS * ROUNDS + kind * ROUNDS + t) * R + (row & 3)
+    gather[...] = jnp.where(column == source, 1.0, 0.0).astype(bf16)
+
+
+def projected_kernel(received, queries, hidden, chosen, w_out, copies):
+    peers = received.shape[0]
+    tails = tails_of(received)
+    fresh = dot(chosen[...], tails.reshape(peers * 8, 128).astype(bf16)).astype(bf16)
+    maxima, totals = stats_of(tails[:, 0])
     parts = []
     for b in range(BATCH):
-        groups = [q[t, b, 0] for q in (queries_draft, queries_verify) for t in range(ROUNDS)]
-        queries = dot(order, jnp.concatenate(groups, axis=0)).astype(bf16)
-        kept = jnp.where(written == 0, accepted[0, b], jnp.where(written == 1, accepted[1, b], 0))
-        visible = itself | (earlier & (token < kept))
-        scores = jnp.where(visible, dot_rows(queries, fresh[b * 32 : b * 32 + 16]) * SCALE, NEG)
+        masked = hidden[b]
+        scores = dot_rows(queries[b], fresh[b * 32 : b * 32 + 16]) * SCALE
+        scores = jnp.where(masked == 0.0, scores, NEG)
         new_highest = jnp.max(scores, axis=1, keepdims=True)
-        weights = jnp.where(visible, jnp.exp(scores - new_highest), 0.0).astype(bf16)
+        weights = jnp.exp(scores - new_highest).astype(bf16)
         new_total = jnp.sum(weights.astype(f32), axis=1, keepdims=True)
         new_sums = dot(weights, fresh[b * 32 + 16 : b * 32 + 32])
         of_b = range(b, peers, BATCH)
@@ -387,17 +397,11 @@
         copies[k] = out
 
 
-def summed_kernel(received, out):
+def summed_kernel(received, gather, out):
     total = received[0].astype(f32)
     for k in range(1, received.shape[0]):
         total = total + received[k].astype(f32)
-    row = lax.broadcasted_iota(jnp.int32, (TOKENS, TOKENS), 0)
-    column = lax.broadcasted_iota(jnp.int32, (TOKENS, TOKENS), 1)
-    at = row >> 2
-    t, kind, b = at >> 3, (at >> 2) & 1, at & 3
-    source = (b * KINDS * ROUNDS + kind * ROUNDS + t) * R + (row & 3)
-    order = jnp.where(column == source, 1.0, 0.0).astype(bf16)
-    ordered = dot(order, total.astype(bf16)).astype(bf16)
+    ordered = dot(gather[...], total.astype(bf16)).astype(bf16)
     out[...] = ordered.reshape(out.shape)
 
 
@@ -436,6 +440,21 @@
         *scales,
     ).reshape(peers, MESSAGE, HD)
     received = lax.all_to_all(message, "seq", 0, 0, tiled=True)
+    shapes = (
+        ((BATCH, KINDS * ROWS, HD), bf16),
+        ((BATCH, KINDS * ROWS, 16), f32),
+        ((BATCH * 2 * 16, peers * 8), bf16),
+        ((TOKENS, TOKENS), bf16),
+    )
+    queries, hidden, chosen, gather = pl.pallas_call(
+        prepared_kernel,
+        out_shape=[jax.ShapeDtypeStruct(*shape) for shape in shapes],
+        in_specs=[pl.BlockSpec(memory_space=pl.ANY), pl.BlockSpec(memory_space=pltpu.SMEM)] + in_vmem(2),
+        out_specs=in_vmem(len(shapes)),
+        compiler_params=params,
+        cost_estimate=pl.CostEstimate(flops=40_000_000, bytes_accessed=4_000_000, transcendentals=0),
+        name="prepared",
+    )(message, accepted, queries_draft, queries_verify)
     copies = pl.pallas_call(
         joined_kernel,
         out_shape=jax.ShapeDtypeStruct((peers, MESSAGE, HD), bf16),
@@ -448,20 +467,20 @@
     copies = pl.pallas_call(
         projected_kernel,
         out_shape=jax.ShapeDtypeStruct((heads, TOKENS, w_out.shape[1]), bf16),
-        in_specs=[pl.BlockSpec(memory_space=pltpu.SMEM)] + in_vmem(4),
+        in_specs=in_vmem(5),
         out_specs=pl.BlockSpec(memory_space=pltpu.VMEM),
         compiler_params=params,
         name="projected",
-    )(accepted, received, queries_draft, queries_verify, w_out)
+    )(received, queries, hidden, chosen, w_out)
     received = lax.all_to_all(copies, "tp", 0, 0, tiled=True)
     return pl.pallas_call(
         summed_kernel,
         out_shape=jax.ShapeDtypeStruct((ROUNDS, KINDS, BATCH * R, w_out.shape[1]), bf16),
-        in_specs=in_vmem(1),
+        in_specs=in_vmem(2),
         out_specs=pl.BlockSpec(memory_space=pltpu.VMEM),
         compiler_params=params,
         name="summed",
-    )(received)
+    )(received, gather)
 
 
 def solution(mesh):

time: 62 us -> 61.8 us (level)
  blocking collectives: 50.8 us -> 37.1 us
  waiting for transfers between devices: 0 us -> 9.46 us
  starting transfers between devices: 0 us -> 4.77 us
  Pallas kernels: 11 us -> 10.2 us
    all_to_all x1 -> x0, blocking collectives: 15 us -> none  [per_device(): received = lax.all_to_all(copies, 'seq', 0, 0, tiled=True)]
    all_to_all x0 -> x1, waiting for transfers between devices: none -> 9.46 us  [per_device(): received = lax.all_to_all(copies, 'seq', 0, 0, tiled=True)]
    all_to_all x0 -> x1, starting transfers between devices: none -> 4.77 us  [per_device(): received = lax.all_to_all(copies, 'seq', 0, 0, tiled=True)]
    all_to_all x1, blocking collectives: 19.7 us -> 20.9 us  [per_device(): received = lax.all_to_all(message, 'seq', 0, 0, tiled=True)]
    pallas_call x1, Pallas kernels: 2.36 us -> 1.13 us  [per_device(): pl.pallas_call(projected_kernel, out_shape=jax.ShapeDtypeStruct((heads, T...]
    pallas_call x1, Pallas kernels: 7.28 us -> 6.13 us  [partials(): pl.pallas_call(partials_kernel, out_shape=jax.ShapeDtypeStruct((GROUP, BA...]
    pallas_call x0 -> x1, Pallas kernels: none -> 0.9 us  [per_device(): pl.pallas_call(prepared_kernel, out_shape=[jax.ShapeDtypeStruct(*shape) f...]
    pallas_call x1, Pallas kernels: 0.5 us -> 1.21 us  [per_device(): pl.pallas_call(joined_kernel, out_shape=jax.ShapeDtypeStruct((peers, MESS...]
  transfers between devices with their start and end apart: 0 -> 1, of which waited for: 0 -> 1; matrix products, arithmetic and copies ran while one was open for 0% -> 0% of each run, Pallas kernels for 0% -> 1%
where the time goes in v5:
time: 61.8 us; the launch traced here: 61.5 us
  blocking collectives  37.1 us (60%)
  Pallas kernels  10.2 us (17%)
  waiting for transfers between devices  9.46 us (15%)
  starting transfers between devices  4.77 us (8%)
    all_to_all x1, blocking collectives, per_device(): received = lax.all_to_all(message, 'seq', 0, 0, tiled=True)  20.9 us
    all_to_all x1, blocking collectives, per_device(): received = lax.all_to_all(copies, 'tp', 0, 0, tiled=True)  16.1 us
    all_to_all x1, waiting for transfers between devices, per_device(): received = lax.all_to_all(copies, 'seq', 0, 0, tiled=True)  9.46 us
    pallas_call x1, Pallas kernels, partials(): pl.pallas_call(partials_kernel, out_shape=jax.ShapeDtypeStruct((GROUP, BA...  6.13 us
    all_to_all x1, starting transfers between devices, per_device(): received = lax.all_to_all(copies, 'seq', 0, 0, tiled=True)  4.77 us
  transfers between devices with their start and end apart: 1, of which 1 were waited for; matrix products, arithmetic and copies ran while one was open for 0% of the time, Pallas kernels for 1%

profile of v5, /device:TPU:1, one launch (start us, length us, event | category | flops | bytes accessed | tf_op | source)
XLA Modules:
  0.0 61.5 jit_solution(6463812194090775137)
XLA Ops:
  0.0 0.0 copy-start.1
  0.0 0.0 copy-start.2
  0.0 0.0 copy-start.3
  0.0 6.1 %partials.1 = bf16[8,4,32,128]{3,2,1,0:T(8,128)(2,1)S(1)} custom-call(s32[4]{0:T(128)} %lengths_hbm.1, bf16[3,16,256]{2,1,0:T(8,128)(2,1)} %hidden_hbm.1, bf16[256,256]{1,0:T(8,128)(2,1)} %bitcast.6, bf16[3,4,1,32,128]{4,3,2,1,0:T(8,128)(2,1)} %queries_draft.1, bf16[3,4,1,32,128]{4,3,2,1,0:T(8,128)(2,1)} %queries_verify.1, ...), custom_call_target="tpu_custom_call" | custom-call | tf_op jit(solution)/shard_map/partials/pallas_call | solution.py:287
  6.1 0.0 copy-start
  6.2 20.9 %all_to_all.15.received = bf16[32,32,128]{2,1,0:T(8,128)(2,1)S(1)} all-to-all(bf16[32,32,128]{2,1,0:T(8,128)(2,1)S(1)} %bitcast.4), channel_id=1, replica_groups=mesh['seq'=32,'tp'=8] {'seq'}, dimensions={0} | all-to-all | bytes 524288 | tf_op jit(solution)/shard_map/all_to_all | solution.py:442
  27.1 1.2 %joined.1 = bf16[32,32,128]{2,1,0:T(8,128)(2,1)} custom-call(bf16[32,32,128]{2,1,0:T(8,128)(2,1)S(1)} %all_to_all.15.received), custom_call_target="tpu_custom_call" | custom-call | tf_op jit(solution)/shard_map/joined/pallas_call | solution.py:458
  28.3 4.8 %all-to-all-start.1 = ((bf16[32,32,128]{2,1,0:T(8,128)(2,1)}), bf16[32,32,128]{2,1,0:T(8,128)(2,1)S(1)}, u32[]{:S(2)}, u32[]{:S(2)}) async-start(bf16[32,32,128]{2,1,0:T(8,128)(2,1)} %joined.1), calls=%async_computation.1 | async-start | bytes 524288 | tf_op jit(solution)/shard_map/all_to_all | solution.py:466
  33.1 0.0 copy-done.1
  33.1 0.0 copy-done.2
  33.1 0.0 copy-done.3
  33.1 0.9 %prepared.1 = (bf16[4,192,128]{2,1,0:T(8,128)(2,1)S(1)}, f32[4,192,16]{2,1,0:T(8,128)S(1)}, bf16[128,256]{1,0:T(8,128)(2,1)S(1)}, bf16[96,96]{1,0:T(8,128)(2,1)S(1)}) custom-call(bf16[32,32,128]{2,1,0:T(8,128)(2,1)S(1)} %bitcast.5, s32[2,4]{1,0:T(2,128)S(1)} %copy-done.3, bf16[3,4,1,32,128]{4,3,2,1,0:T(8,128)(2,1)S(1)} %copy-done.1, ...), custom_call_target="tpu_custom_call" | custom-call | flops 40000000 | bytes 4000000 | tf_op jit(solution)/shard_map/prepared/pallas_call | solution.py:449
  34.0 9.5 %all-to-all-done.1.received = bf16[32,32,128]{2,1,0:T(8,128)(2,1)S(1)} async-done(((bf16[32,32,128]{2,1,0:T(8,128)(2,1)}), bf16[32,32,128]{2,1,0:T(8,128)(2,1)S(1)}, u32[]{:S(2)}, u32[]{:S(2)}) %all-to-all-start.1) | async-done | bytes 262176 | tf_op jit(solution)/shard_map/all_to_all | solution.py:466
  43.5 0.0 copy-done
  43.5 1.1 %projected.1 = bf16[8,96,256]{2,1,0:T(8,128)(2,1)S(1)} custom-call(bf16[32,32,128]{2,1,0:T(8,128)(2,1)S(1)} %all-to-all-done.1.received, bf16[4,192,128]{2,1,0:T(8,128)(2,1)S(1)} %get-tuple-element.9.queries, f32[4,192,16]{2,1,0:T(8,128)S(1)} %get-tuple-element.10.hidden, bf16[128,256]{1,0:T(8,128)(2,1)S(1)} %get-tuple-element.11.chosen, ...), custom_call_target="tpu_custom_call" | custom-call | tf_op jit(solution)/shard_map/projected/pallas_call | solution.py:467
  44.6 16.1 %all_to_all.16.received = bf16[8,96,256]{2,1,0:T(8,128)(2,1)S(1)} all-to-all(bf16[8,96,256]{2,1,0:T(8,128)(2,1)S(1)} %projected.1), channel_id=1, replica_groups=mesh['seq'=32,'tp'=8] {'tp'}, dimensions={0} | all-to-all | bytes 786432 | tf_op jit(solution)/shard_map/all_to_all | solution.py:475
  60.7 0.8 %summed.1 = bf16[3,2,16,256]{3,2,1,0:T(8,128)(2,1)} custom-call(bf16[8,96,256]{2,1,0:T(8,128)(2,1)S(1)} %all_to_all.16.received, bf16[96,96]{1,0:T(8,128)(2,1)S(1)} %get-tuple-element.12.gather), custom_call_target="tpu_custom_call" | custom-call | tf_op jit(solution)/shard_map/summed/pallas_call | solution.py:476
Async XLA Ops:
  0.0 33.1 %copy-start.1 = (bf16[3,4,1,32,128]{4,3,2,1,0:T(8,128)(2,1)S(1)}, bf16[3,4,1,32,128]{4,3,2,1,0:T(8,128)(2,1)}, u32[]{:S(2)}) copy-start(bf16[3,4,1,32,128]{4,3,2,1,0:T(8,128)(2,1)} %queries_draft.1) | copy-start | bytes 294916
  0.0 33.1 %copy-start.2 = (bf16[3,4,1,32,128]{4,3,2,1,0:T(8,128)(2,1)S(1)}, bf16[3,4,1,32,128]{4,3,2,1,0:T(8,128)(2,1)}, u32[]{:S(2)}) copy-start(bf16[3,4,1,32,128]{4,3,2,1,0:T(8,128)(2,1)} %queries_verify.1) | copy-start | bytes 294916
  0.0 33.1 %copy-start.3 = (s32[2,4]{1,0:T(2,128)S(1)}, s32[2,4]{1,0:T(2,128)}, u32[]{:S(2)}) copy-start(s32[2,4]{1,0:T(2,128)} %accepted.1) | copy-start | bytes 100
  6.1 37.3 %copy-start = (bf16[1024,256]{1,0:T(8,128)(2,1)S(1)}, bf16[1024,256]{1,0:T(8,128)(2,1)}, u32[]{:S(2)}) copy-start(bf16[1024,256]{1,0:T(8,128)(2,1)} %w_out.1) | copy-start | bytes 1572868
  28.3 15.2 %all-to-all-start.1 = ((bf16[32,32,128]{2,1,0:T(8,128)(2,1)}), bf16[32,32,128]{2,1,0:T(8,128)(2,1)S(1)}, u32[]{:S(2)}, u32[]{:S(2)}) async-start(bf16[32,32,128]{2,1,0:T(8,128)(2,1)} %joined.1), calls=%async_computation.1 | async-start | bytes 524288 | tf_op jit(solution)/shard_map/all_to_all | solution.py:466

commit v6 on v5

--- a/solution.py
+++ b/solution.py
@@ -23,6 +23,7 @@
 TAIL = SHARE
 PIECE = 3
 MESSAGE = SHARE + 8
+CHOSEN = (BATCH * 2 * 16, GROUP * BATCH * 8)
 STEP = 512
 FEW = 256
 VMEM_LIMIT = 48 * 1024 * 1024
@@ -54,6 +55,27 @@
     column = lax.broadcasted_iota(jnp.int32, (KINDS * ROWS, KINDS * ROWS), 1)
     target = ((column >> 2) & 7) * SHARE + ((column >> 5) << 2) + (column & 3)
     return jnp.where(row == target, 1.0, 0.0).astype(bf16)
+
+
+def fresh_selection():
+    row = lax.broadcasted_iota(jnp.int32, CHOSEN, 0)
+    column = lax.broadcasted_iota(jnp.int32, CHOSEN, 1)
+    within = (column & 7) - 1
+    source = (column >> 3) * PIECE + within
+    kv = jnp.where(source >= TOKENS // KINDS, 1, 0)
+    token = source - kv * (TOKENS // KINDS)
+    target = ((token >> 2) & 3) * 32 + kv * 16 + ((token >> 4) << 2) + (token & 3)
+    taken = (within >= 0) & (within < PIECE) & (row == target)
+    return jnp.where(taken, 1.0, 0.0).astype(bf16)
+
+
+def token_order():
+    row = lax.broadcasted_iota(jnp.int32, (TOKENS, TOKENS), 0)
+    column = lax.broadcasted_iota(jnp.int32, (TOKENS, TOKENS), 1)
+    at = row >> 2
+    t, kind, b = at >> 3, (at >> 2) & 1, at & 3
+    source = (b * KINDS * ROUNDS + kind * ROUNDS + t) * R + (row & 3)
+    return jnp.where(column == source, 1.0, 0.0).astype(bf16)
 
 
 def stats_spread(maxima, totals, place):
@@ -106,6 +128,7 @@
 
 def partials_kernel(
     lengths_hbm,
+    accepted_hbm,
     hidden_hbm,
     w_kv_hbm,
     queries_draft_hbm,
@@ -117,7 +140,12 @@
     key_scales_hbm,
     value_scales_hbm,
     message,
+    by_head_queries,
+    unseen,
+    chosen,
+    gather,
     lengths,
+    accepted,
     hidden,
     w_kv,
     queries_draft,
@@ -129,8 +157,6 @@
     key_scales,
     value_scales,
     scores,
-    sums,
-    stats,
     order,
     tails,
     small_sems,
@@ -143,6 +169,7 @@
         for k, (source, target) in enumerate(
             (
                 (lengths_hbm, lengths),
+                (accepted_hbm, accepted),
                 (queries_draft_hbm, queries_draft),
                 (queries_verify_hbm, queries_verify),
                 (key_scales_hbm, key_scales),
@@ -154,6 +181,9 @@
     ]
     for copy in small:
         copy.start()
+    order[...] = by_head()
+    chosen[...] = fresh_selection()
+    gather[...] = token_order()
     small[0].wait()
     first = lax.axis_index("seq") * local_len
 
@@ -187,7 +217,6 @@
             for copy in cache_copies(b, few):
                 copy.start()
 
-    order[...] = by_head()
     for copy in small[1:]:
         copy.wait()
     part = dot(hidden[...].reshape(ROUNDS * BATCH * R, hidden.shape[2]), w_kv[...])
@@ -210,6 +239,22 @@
     column = lax.broadcasted_iota(jnp.int32, (GROUP, KINDS * ROWS), 1)
     of_head = jnp.where(((column >> 2) & 7) == row, 1.0, 0.0).astype(bf16)
     first_row = lax.broadcasted_iota(jnp.int32, (GROUP, 8, 128), 1) == 0
+
+    row = lax.broadcasted_iota(jnp.int32, (KINDS * ROWS, 16), 0)
+    column = lax.broadcasted_iota(jnp.int32, (KINDS * ROWS, 16), 1)
+    turn = (row - ((row * 171) >> 12) * SHARE) >> 2
+    turn = jnp.where(turn >= ROUNDS, turn - ROUNDS, turn)
+    written, token = column >> 2, column & 3
+    itself = (written == turn) & (token <= (row & 3))
+    earlier = written < turn
+    none = jnp.where(lax.broadcasted_iota(jnp.int32, (GROUP, 8, 128), 2) < SHARE, NEG, 0.0)
+    for b in range(BATCH):
+        groups = [q[t, b, 0] for q in (queries_draft, queries_verify) for t in range(ROUNDS)]
+        by_head_queries[b] = dot(order[...], jnp.concatenate(groups, axis=0)).astype(bf16)
+        kept = jnp.where(written == 0, accepted[0, b], jnp.where(written == 1, accepted[1, b], 0))
+        unseen[b] = jnp.where(itself | (earlier & (token < kept)), 0.0, NEG)
+        tail = jnp.where(first_row, none, tails[:, b])
+        message[:, b] = jnp.concatenate([jnp.zeros((GROUP, SHARE, HD), f32), tail], axis=1).astype(bf16)
 
     def sequence(b, _):
         usable = usable_of(b)
@@ -248,15 +293,11 @@
                 scores,
                 positions,
             )
-            sums[b, :ROWS] = weighted[:ROWS, :HD].astype(bf16)
-            sums[b, ROWS:] = weighted[ROWS:, HD:].astype(bf16)
-            stats[b] = stats_spread(maxima, totals, place).astype(bf16)
-
-        @pl.when(usable == 0)
-        def _():
-            sums[b] = jnp.zeros((KINDS * ROWS, HD), bf16)
-            none = jnp.zeros((KINDS * ROWS, 1), f32)
-            stats[b] = stats_spread(none + NEG, none, place).astype(bf16)
+            sums = jnp.concatenate([weighted[:ROWS, :HD], weighted[ROWS:, HD:]], axis=0).astype(bf16)
+            stats = stats_spread(maxima, totals, place).astype(bf16)
+            ordered = dot(order[...], sums).reshape(GROUP, SHARE, HD)
+            tail = jnp.where(first_row, dot(of_head, stats).reshape(GROUP, 1, 128), tails[:, b])
+            message[:, b] = jnp.concatenate([ordered, tail], axis=1).astype(bf16)
 
         @pl.when((usable > 0) & (usable <= few))
         def _():
@@ -273,24 +314,26 @@
         return 0
 
     lax.fori_loop(0, BATCH, sequence, 0)
-    for b in range(BATCH):
-        ordered = dot(order[...], sums[b]).reshape(GROUP, SHARE, HD)
-        head_stats = dot(of_head, stats[b]).reshape(GROUP, 1, 128)
-        tail = jnp.where(first_row, head_stats, tails[:, b])
-        message[:, b] = jnp.concatenate([ordered, tail], axis=1).astype(bf16)
-
-
-def partials(lengths, *arrays):
+
+
+def partials(lengths, accepted, *arrays):
     local_len = arrays[4].shape[2]
     hidden, w_kv, queries = arrays[:3]
     blocks = local_len // 128
     return pl.pallas_call(
         partials_kernel,
-        out_shape=jax.ShapeDtypeStruct((GROUP, BATCH, MESSAGE, HD), bf16),
-        in_specs=[pl.BlockSpec(memory_space=pltpu.HBM)] * (1 + len(arrays)),
-        out_specs=pl.BlockSpec(memory_space=pltpu.VMEM),
+        out_shape=[
+            jax.ShapeDtypeStruct((GROUP, BATCH, MESSAGE, HD), bf16),
+            jax.ShapeDtypeStruct((BATCH, KINDS * ROWS, HD), bf16),
+            jax.ShapeDtypeStruct((BATCH, KINDS * ROWS, 16), f32),
+            jax.ShapeDtypeStruct(CHOSEN, bf16),
+            jax.ShapeDtypeStruct((TOKENS, TOKENS), bf16),
+        ],
+        in_specs=[pl.BlockSpec(memory_space=pltpu.HBM)] * (2 + len(arrays)),
+        out_specs=[pl.BlockSpec(memory_space=pltpu.VMEM)] * 5,
         scratch_shapes=[
             pltpu.SMEM((BATCH,), jnp.int32),
+            pltpu.SMEM(accepted.shape, jnp.int32),
             pltpu.VMEM(hidden.shape, bf16),
             pltpu.VMEM(w_kv.shape, bf16),
             pltpu.VMEM(queries.shape, bf16),
@@ -302,16 +345,14 @@
             pltpu.VMEM((BATCH, blocks, 128), f32),
             pltpu.VMEM((BATCH, blocks, 128), f32),
             pltpu.VMEM((KINDS * ROWS, local_len), f32),
-            pltpu.VMEM((BATCH, KINDS * ROWS, HD), bf16),
-            pltpu.VMEM((BATCH, KINDS * ROWS, 128), bf16),
             pltpu.VMEM((KINDS * ROWS, KINDS * ROWS), bf16),
             pltpu.VMEM((GROUP, BATCH, 8, 128), f32),
-            pltpu.SemaphoreType.DMA((7,)),
+            pltpu.SemaphoreType.DMA((8,)),
             pltpu.SemaphoreType.DMA((BATCH, 4)),
         ],
         compiler_params=pltpu.CompilerParams(vmem_limit_bytes=VMEM_LIMIT),
         name="partials",
-    )(*(pltpu.with_memory_space_constraint(x, pltpu.HBM) for x in (lengths, *arrays)))
+    )(*(pltpu.with_memory_space_constraint(x, pltpu.HBM) for x in (lengths, accepted, *arrays)))
 
 
 def joined_kernel(received, copies):
@@ -335,47 +376,15 @@
         copies[s] = block
 
 
-def prepared_kernel(_, accepted, queries_draft, queries_verify, queries, hidden, chosen, gather):
-    order = by_head()
-    row = lax.broadcasted_iota(jnp.int32, (KINDS * ROWS, 16), 0)
-    column = lax.broadcasted_iota(jnp.int32, (KINDS * ROWS, 16), 1)
-    turn = (row - ((row * 171) >> 12) * SHARE) >> 2
-    turn = jnp.where(turn >= ROUNDS, turn - ROUNDS, turn)
-    written, token = column >> 2, column & 3
-    itself = (written == turn) & (token <= (row & 3))
-    earlier = written < turn
-    for b in range(BATCH):
-        groups = [q[t, b, 0] for q in (queries_draft, queries_verify) for t in range(ROUNDS)]
-        queries[b] = dot(order, jnp.concatenate(groups, axis=0)).astype(bf16)
-        kept = jnp.where(written == 0, accepted[0, b], jnp.where(written == 1, accepted[1, b], 0))
-        hidden[b] = jnp.where(itself | (earlier & (token < kept)), 0.0, NEG)
-    row = lax.broadcasted_iota(jnp.int32, chosen.shape, 0)
-    column = lax.broadcasted_iota(jnp.int32, chosen.shape, 1)
-    within = (column & 7) - 1
-    source = (column >> 3) * PIECE + within
-    kv = jnp.where(source >= TOKENS // KINDS, 1, 0)
-    token = source - kv * (TOKENS // KINDS)
-    target = ((token >> 2) & 3) * 32 + kv * 16 + ((token >> 4) << 2) + (token & 3)
-    taken = (within >= 0) & (within < PIECE) & (row == target)
-    chosen[...] = jnp.where(taken, 1.0, 0.0).astype(bf16)
-    row = lax.broadcasted_iota(jnp.int32, gather.shape, 0)
-    column = lax.broadcasted_iota(jnp.int32, gather.shape, 1)
-    at = row >> 2
-    t, kind, b = at >> 3, (at >> 2) & 1, at & 3
-    source = (b * KINDS * ROUNDS + kind * ROUNDS + t) * R + (row & 3)
-    gather[...] = jnp.where(column == source, 1.0, 0.0).astype(bf16)
-
-
-def projected_kernel(received, queries, hidden, chosen, w_out, copies):
+def projected_kernel(received, queries, unseen, chosen, w_out, copies):
     peers = received.shape[0]
     tails = tails_of(received)
     fresh = dot(chosen[...], tails.reshape(peers * 8, 128).astype(bf16)).astype(bf16)
     maxima, totals = stats_of(tails[:, 0])
     parts = []
     for b in range(BATCH):
-        masked = hidden[b]
         scores = dot_rows(queries[b], fresh[b * 32 : b * 32 + 16]) * SCALE
-        scores = jnp.where(masked == 0.0, scores, NEG)
+        scores = jnp.where(unseen[b] == 0.0, scores, NEG)
         new_highest = jnp.max(scores, axis=1, keepdims=True)
         weights = jnp.exp(scores - new_highest).astype(bf16)
         new_total = jnp.sum(weights.astype(f32), axis=1, keepdims=True)
@@ -427,8 +436,9 @@
     peers, heads = lax.axis_size("seq"), lax.axis_size("tp")
     params = pltpu.CompilerParams(vmem_limit_bytes=VMEM_LIMIT)
     scales = [x.reshape(BATCH, -1, 128) for x in (key_scales, value_scales)]
-    message = partials(
+    message, queries, unseen, chosen, gather = partials(
         lengths,
+        accepted,
         hidden_new,
         w_kv.reshape(w_kv.shape[0], -1),
         queries_draft,
@@ -438,23 +448,8 @@
         key_levels,
         value_levels,
         *scales,
-    ).reshape(peers, MESSAGE, HD)
-    received = lax.all_to_all(message, "seq", 0, 0, tiled=True)
-    shapes = (
-        ((BATCH, KINDS * ROWS, HD), bf16),
-        ((BATCH, KINDS * ROWS, 16), f32),
-        ((BATCH * 2 * 16, peers * 8), bf16),
-        ((TOKENS, TOKENS), bf16),
     )
-    queries, hidden, chosen, gather = pl.pallas_call(
-        prepared_kernel,
-        out_shape=[jax.ShapeDtypeStruct(*shape) for shape in shapes],
-        in_specs=[pl.BlockSpec(memory_space=pl.ANY), pl.BlockSpec(memory_space=pltpu.SMEM)] + in_vmem(2),
-        out_specs=in_vmem(len(shapes)),
-        compiler_params=params,
-        cost_estimate=pl.CostEstimate(flops=40_000_000, bytes_accessed=4_000_000, transcendentals=0),
-        name="prepared",
-    )(message, accepted, queries_draft, queries_verify)
+    received = lax.all_to_all(message.reshape(peers, MESSAGE, HD), "seq", 0, 0, tiled=True)
     copies = pl.pallas_call(
         joined_kernel,
         out_shape=jax.ShapeDtypeStruct((peers, MESSAGE, HD), bf16),
@@ -471,7 +466,7 @@
         out_specs=pl.BlockSpec(memory_space=pltpu.VMEM),
         compiler_params=params,
         name="projected",
-    )(received, queries, hidden, chosen, w_out)
+    )(received, queries, unseen, chosen, w_out)
     received = lax.all_to_all(copies, "tp", 0, 0, tiled=True)
     return pl.pallas_call(
         summed_kernel,

time: 61.8 us -> 60.5 us (0.979)
  blocking collectives: 37.1 us -> 50.4 us
  waiting for transfers between devices: 9.46 us -> 0 us
  starting transfers between devices: 4.77 us -> 0 us
    all_to_all x1 -> x2, blocking collectives: 20.9 us -> 34.3 us  [the longest x1 19.3 us: per_device(): lax.all_to_all(message.reshape(peers, MESSAGE, HD), 'seq', 0, 0, tiled=True)]
    all_to_all x1 -> x0, waiting for transfers between devices: 9.46 us -> none  [per_device(): received = lax.all_to_all(copies, 'seq', 0, 0, tiled=True)]
    all_to_all x1 -> x0, starting transfers between devices: 4.77 us -> none  [per_device(): received = lax.all_to_all(copies, 'seq', 0, 0, tiled=True)]
    pallas_call x1, Pallas kernels: 1.21 us -> 0.5 us  [per_device(): pl.pallas_call(joined_kernel, out_shape=jax.ShapeDtypeStruct((peers, MESS...]
    pallas_call x2 -> x1, Pallas kernels: 7.04 us -> 7.47 us  [partials(): pl.pallas_call(partials_kernel, out_shape=[jax.ShapeDtypeStruct((GROUP, B...]
  transfers between devices with their start and end apart: 1 -> 0, of which waited for: 1 -> 0; matrix products, arithmetic and copies ran while one was open for 0% -> 0% of each run, Pallas kernels for 1% -> 0%
where the time goes in v6:
time: 60.5 us; the launch traced here: 60.3 us
  blocking collectives  50.4 us (83%)
  Pallas kernels  9.9 us (16%)
    all_to_all x1, blocking collectives, per_device(): lax.all_to_all(message.reshape(peers, MESSAGE, HD), 'seq', 0, 0, tiled=True)  19.3 us
    all_to_all x1, blocking collectives, per_device(): received = lax.all_to_all(copies, 'tp', 0, 0, tiled=True)  16.1 us
    all_to_all x1, blocking collectives, per_device(): received = lax.all_to_all(copies, 'seq', 0, 0, tiled=True)  15 us
    pallas_call x1, Pallas kernels, partials(): pl.pallas_call(partials_kernel, out_shape=[jax.ShapeDtypeStruct((GROUP, B...  7.47 us

profile of v6, /device:TPU:1, one launch (start us, length us, event | category | flops | bytes accessed | tf_op | source)
XLA Modules:
  0.0 60.3 jit_solution(6508114888895891013)
XLA Ops:
  0.0 0.0 copy-start
  0.0 7.5 %partials.1 = (bf16[8,4,32,128]{3,2,1,0:T(8,128)(2,1)S(1)}, bf16[4,192,128]{2,1,0:T(8,128)(2,1)S(1)}, f32[4,192,16]{2,1,0:T(8,128)S(1)}, bf16[128,256]{1,0:T(8,128)(2,1)S(1)}, bf16[96,96]{1,0:T(8,128)(2,1)S(1)}) custom-call(s32[4]{0:T(128)} %lengths_hbm.1, s32[2,4]{1,0:T(2,128)} %accepted_hbm.1, bf16[3,16,256]{2,1,0:T(8,128)(2,1)} %hidden_hbm.1, ...), custom_call_target="tpu_custom_call" | custom-call | tf_op jit(solution)/shard_map/partials/pallas_call | solution.py:323
  7.5 19.3 %all_to_all.15.received = bf16[32,32,128]{2,1,0:T(8,128)(2,1)S(1)} all-to-all(bf16[32,32,128]{2,1,0:T(8,128)(2,1)S(1)} %bitcast.4), channel_id=1, replica_groups=mesh['seq'=32,'tp'=8] {'seq'}, dimensions={0} | all-to-all | bytes 524288 | tf_op jit(solution)/shard_map/all_to_all | solution.py:452
  26.8 0.5 joined.1
  27.3 15.0 %all_to_all.16.received = bf16[32,32,128]{2,1,0:T(8,128)(2,1)S(1)} all-to-all(bf16[32,32,128]{2,1,0:T(8,128)(2,1)S(1)} %joined.1), channel_id=1, replica_groups=mesh['seq'=32,'tp'=8] {'seq'}, dimensions={0} | all-to-all | bytes 524288 | tf_op jit(solution)/shard_map/all_to_all | solution.py:461
  42.3 0.0 copy-done
  42.3 1.1 %projected.1 = bf16[8,96,256]{2,1,0:T(8,128)(2,1)S(1)} custom-call(bf16[32,32,128]{2,1,0:T(8,128)(2,1)S(1)} %all_to_all.16.received, bf16[4,192,128]{2,1,0:T(8,128)(2,1)S(1)} %get-tuple-element.11.queries, f32[4,192,16]{2,1,0:T(8,128)S(1)} %get-tuple-element.12.unseen, bf16[128,256]{1,0:T(8,128)(2,1)S(1)} %get-tuple-element.13.chosen, ...), custom_call_target="tpu_custom_call" | custom-call | tf_op jit(solution)/shard_map/projected/pallas_call | solution.py:462
  43.4 16.1 %all_to_all.17.received = bf16[8,96,256]{2,1,0:T(8,128)(2,1)S(1)} all-to-all(bf16[8,96,256]{2,1,0:T(8,128)(2,1)S(1)} %projected.1), channel_id=1, replica_groups=mesh['seq'=32,'tp'=8] {'tp'}, dimensions={0} | all-to-all | bytes 786432 | tf_op jit(solution)/shard_map/all_to_all | solution.py:470
  59.5 0.8 %summed.1 = bf16[3,2,16,256]{3,2,1,0:T(8,128)(2,1)} custom-call(bf16[8,96,256]{2,1,0:T(8,128)(2,1)S(1)} %all_to_all.17.received, bf16[96,96]{1,0:T(8,128)(2,1)S(1)} %get-tuple-element.14.gather), custom_call_target="tpu_custom_call" | custom-call | tf_op jit(solution)/shard_map/summed/pallas_call | solution.py:471
Async XLA Ops:
  0.0 42.3 %copy-start = (bf16[1024,256]{1,0:T(8,128)(2,1)S(1)}, bf16[1024,256]{1,0:T(8,128)(2,1)}, u32[]{:S(2)}) copy-start(bf16[1024,256]{1,0:T(8,128)(2,1)} %w_out.1) | copy-start | bytes 1572868

commit v7 on v6

--- a/solution.py
+++ b/solution.py
@@ -69,9 +69,10 @@
     return jnp.where(taken, 1.0, 0.0).astype(bf16)
 
 
-def token_order():
-    row = lax.broadcasted_iota(jnp.int32, (TOKENS, TOKENS), 0)
-    column = lax.broadcasted_iota(jnp.int32, (TOKENS, TOKENS), 1)
+def token_order(shares):
+    row = lax.broadcasted_iota(jnp.int32, (TOKENS, shares * TOKENS), 0)
+    column = lax.broadcasted_iota(jnp.int32, (1, shares * TOKENS), 1)
+    column = column - TOKENS * sum(jnp.where(column >= k * TOKENS, 1, 0) for k in range(1, shares))
     at = row >> 2
     t, kind, b = at >> 3, (at >> 2) & 1, at & 3
     source = (b * KINDS * ROUNDS + kind * ROUNDS + t) * R + (row & 3)
@@ -183,7 +184,7 @@
         copy.start()
     order[...] = by_head()
     chosen[...] = fresh_selection()
-    gather[...] = token_order()
+    gather[...] = token_order(gather.shape[1] // TOKENS)
     small[0].wait()
     first = lax.axis_index("seq") * local_len
 
@@ -327,7 +328,7 @@
             jax.ShapeDtypeStruct((BATCH, KINDS * ROWS, HD), bf16),
             jax.ShapeDtypeStruct((BATCH, KINDS * ROWS, 16), f32),
             jax.ShapeDtypeStruct(CHOSEN, bf16),
-            jax.ShapeDtypeStruct((TOKENS, TOKENS), bf16),
+            jax.ShapeDtypeStruct((TOKENS, lax.axis_size("tp") * TOKENS), bf16),
         ],
         in_specs=[pl.BlockSpec(memory_space=pltpu.HBM)] * (2 + len(arrays)),
         out_specs=[pl.BlockSpec(memory_space=pltpu.VMEM)] * 5,
@@ -407,11 +408,8 @@
 
 
 def summed_kernel(received, gather, out):
-    total = received[0].astype(f32)
-    for k in range(1, received.shape[0]):
-        total = total + received[k].astype(f32)
-    ordered = dot(gather[...], total.astype(bf16)).astype(bf16)
-    out[...] = ordered.reshape(out.shape)
+    shares = received[...].reshape(-1, received.shape[2])
+    out[...] = dot(gather[...], shares).astype(bf16).reshape(out.shape)
 
 
 def in_vmem(count):

time: 60.5 us -> 60.5 us (level)
  no operation moved by 1% of the time
where the time goes in v7:
time: 60.5 us; the launch traced here: 60.3 us
  blocking collectives  50.4 us (83%)
  Pallas kernels  9.93 us (16%)
    all_to_all x1, blocking collectives, per_device(): lax.all_to_all(message.reshape(peers, MESSAGE, HD), 'seq', 0, 0, tiled=True)  19.3 us
    all_to_all x1, blocking collectives, per_device(): received = lax.all_to_all(copies, 'tp', 0, 0, tiled=True)  16.1 us
    all_to_all x1, blocking collectives, per_device(): received = lax.all_to_all(copies, 'seq', 0, 0, tiled=True)  15 us
    pallas_call x1, Pallas kernels, partials(): pl.pallas_call(partials_kernel, out_shape=[jax.ShapeDtypeStruct((GROUP, B...  7.47 us

profile of v7, /device:TPU:1, one launch (start us, length us, event | category | flops | bytes accessed | tf_op | source)
XLA Modules:
  0.0 60.3 jit_solution(17809983666522221364)
XLA Ops:
  0.0 0.0 copy-start
  0.0 7.5 %partials.1 = (bf16[8,4,32,128]{3,2,1,0:T(8,128)(2,1)S(1)}, bf16[4,192,128]{2,1,0:T(8,128)(2,1)S(1)}, f32[4,192,16]{2,1,0:T(8,128)S(1)}, bf16[128,256]{1,0:T(8,128)(2,1)S(1)}, bf16[96,768]{1,0:T(8,128)(2,1)S(1)}) custom-call(s32[4]{0:T(128)} %lengths_hbm.1, s32[2,4]{1,0:T(2,128)} %accepted_hbm.1, bf16[3,16,256]{2,1,0:T(8,128)(2,1)} %hidden_hbm.1, ...), custom_call_target="tpu_custom_call" | custom-call | tf_op jit(solution)/shard_map/partials/pallas_call | solution.py:324
  7.5 19.3 %all_to_all.15.received = bf16[32,32,128]{2,1,0:T(8,128)(2,1)S(1)} all-to-all(bf16[32,32,128]{2,1,0:T(8,128)(2,1)S(1)} %bitcast.4), channel_id=1, replica_groups=mesh['seq'=32,'tp'=8] {'seq'}, dimensions={0} | all-to-all | bytes 524288 | tf_op jit(solution)/shard_map/all_to_all | solution.py:450
  26.8 0.5 joined.1
  27.3 15.0 %all_to_all.16.received = bf16[32,32,128]{2,1,0:T(8,128)(2,1)S(1)} all-to-all(bf16[32,32,128]{2,1,0:T(8,128)(2,1)S(1)} %joined.1), channel_id=1, replica_groups=mesh['seq'=32,'tp'=8] {'seq'}, dimensions={0} | all-to-all | bytes 524288 | tf_op jit(solution)/shard_map/all_to_all | solution.py:459
  42.3 0.0 copy-done
  42.3 1.1 %projected.1 = bf16[8,96,256]{2,1,0:T(8,128)(2,1)S(1)} custom-call(bf16[32,32,128]{2,1,0:T(8,128)(2,1)S(1)} %all_to_all.16.received, bf16[4,192,128]{2,1,0:T(8,128)(2,1)S(1)} %get-tuple-element.11.queries, f32[4,192,16]{2,1,0:T(8,128)S(1)} %get-tuple-element.12.unseen, bf16[128,256]{1,0:T(8,128)(2,1)S(1)} %get-tuple-element.13.chosen, ...), custom_call_target="tpu_custom_call" | custom-call | tf_op jit(solution)/shard_map/projected/pallas_call | solution.py:460
  43.4 16.1 %all_to_all.17.received = bf16[8,96,256]{2,1,0:T(8,128)(2,1)S(1)} all-to-all(bf16[8,96,256]{2,1,0:T(8,128)(2,1)S(1)} %projected.1), channel_id=1, replica_groups=mesh['seq'=32,'tp'=8] {'tp'}, dimensions={0} | all-to-all | bytes 786432 | tf_op jit(solution)/shard_map/all_to_all | solution.py:468
  59.5 0.8 %summed.1 = bf16[3,2,16,256]{3,2,1,0:T(8,128)(2,1)} custom-call(bf16[8,96,256]{2,1,0:T(8,128)(2,1)S(1)} %all_to_all.17.received, bf16[96,768]{1,0:T(8,128)(2,1)S(1)} %get-tuple-element.14.gather), custom_call_target="tpu_custom_call" | custom-call | tf_op jit(solution)/shard_map/summed/pallas_call | solution.py:469
Async XLA Ops:
  0.0 42.3 %copy-start = (bf16[1024,256]{1,0:T(8,128)(2,1)S(1)}, bf16[1024,256]{1,0:T(8,128)(2,1)}, u32[]{:S(2)}) copy-start(bf16[1024,256]{1,0:T(8,128)(2,1)} %w_out.1) | copy-start | bytes 1572868

commit v8 on v6

--- a/solution.py
+++ b/solution.py
@@ -25,7 +25,7 @@
 MESSAGE = SHARE + 8
 CHOSEN = (BATCH * 2 * 16, GROUP * BATCH * 8)
 STEP = 512
-FEW = 256
+FEW = 128
 VMEM_LIMIT = 48 * 1024 * 1024
 
 f32 = jnp.float32
@@ -362,9 +362,10 @@
     highest = jnp.max(maxima, axis=1, keepdims=True)
     factors = jnp.exp(maxima - highest)
     total = jnp.sum(totals * factors, axis=1, keepdims=True)
-    sums = jnp.zeros((SHARE, HD), f32)
+    chains = [jnp.zeros((SHARE, HD), f32)] * 4
     for s in range(peers):
-        sums = sums + factors[:, s : s + 1] * received[s].astype(f32)[:SHARE]
+        chains[s % 4] += factors[:, s : s + 1] * received[s].astype(f32)[:SHARE]
+    sums = (chains[0] + chains[1]) + (chains[2] + chains[3])
     fresh = jnp.sum(tails, axis=0)
     fresh = fresh + jnp.concatenate([fresh[PIECE:], fresh[:PIECE]], axis=0)
     place = lax.broadcasted_iota(jnp.int32, (SHARE, 1), 0)

time: 60.5 us -> 60.5 us (level)
  Pallas kernels: 9.9 us -> 10.6 us
  blocking collectives: 50.4 us -> 49.7 us
    all_to_all x1, blocking collectives: 19.3 us -> 18.6 us  [per_device(): lax.all_to_all(message.reshape(peers, MESSAGE, HD), 'seq', 0, 0, tiled=True)]
    pallas_call x1, Pallas kernels: 7.47 us -> 8.19 us  [partials(): pl.pallas_call(partials_kernel, out_shape=[jax.ShapeDtypeStruct((GROUP, B...]
where the time goes in v8:
time: 60.5 us; the launch traced here: 60.3 us
  blocking collectives  49.7 us (82%)
  Pallas kernels  10.6 us (18%)
    all_to_all x1, blocking collectives, per_device(): lax.all_to_all(message.reshape(peers, MESSAGE, HD), 'seq', 0, 0, tiled=True)  18.6 us
    all_to_all x1, blocking collectives, per_device(): received = lax.all_to_all(copies, 'tp', 0, 0, tiled=True)  16.1 us
    all_to_all x1, blocking collectives, per_device(): received = lax.all_to_all(copies, 'seq', 0, 0, tiled=True)  15 us
    pallas_call x1, Pallas kernels, partials(): pl.pallas_call(partials_kernel, out_shape=[jax.ShapeDtypeStruct((GROUP, B...  8.19 us

profile of v8, /device:TPU:1, one launch (start us, length us, event | category | flops | bytes accessed | tf_op | source)
XLA Modules:
  0.0 60.3 jit_solution(11557755799417162742)
XLA Ops:
  0.0 0.0 copy-start
  0.0 8.2 %partials.1 = (bf16[8,4,32,128]{3,2,1,0:T(8,128)(2,1)S(1)}, bf16[4,192,128]{2,1,0:T(8,128)(2,1)S(1)}, f32[4,192,16]{2,1,0:T(8,128)S(1)}, bf16[128,256]{1,0:T(8,128)(2,1)S(1)}, bf16[96,96]{1,0:T(8,128)(2,1)S(1)}) custom-call(s32[4]{0:T(128)} %lengths_hbm.1, s32[2,4]{1,0:T(2,128)} %accepted_hbm.1, bf16[3,16,256]{2,1,0:T(8,128)(2,1)} %hidden_hbm.1, ...), custom_call_target="tpu_custom_call" | custom-call | tf_op jit(solution)/shard_map/partials/pallas_call | solution.py:323
  8.2 18.6 %all_to_all.15.received = bf16[32,32,128]{2,1,0:T(8,128)(2,1)S(1)} all-to-all(bf16[32,32,128]{2,1,0:T(8,128)(2,1)S(1)} %bitcast.4), channel_id=1, replica_groups=mesh['seq'=32,'tp'=8] {'seq'}, dimensions={0} | all-to-all | bytes 524288 | tf_op jit(solution)/shard_map/all_to_all | solution.py:453
  26.8 0.5 joined.1
  27.3 15.0 %all_to_all.16.received = bf16[32,32,128]{2,1,0:T(8,128)(2,1)S(1)} all-to-all(bf16[32,32,128]{2,1,0:T(8,128)(2,1)S(1)} %joined.1), channel_id=1, replica_groups=mesh['seq'=32,'tp'=8] {'seq'}, dimensions={0} | all-to-all | bytes 524288 | tf_op jit(solution)/shard_map/all_to_all | solution.py:462
  42.3 0.0 copy-done
  42.3 1.1 %projected.1 = bf16[8,96,256]{2,1,0:T(8,128)(2,1)S(1)} custom-call(bf16[32,32,128]{2,1,0:T(8,128)(2,1)S(1)} %all_to_all.16.received, bf16[4,192,128]{2,1,0:T(8,128)(2,1)S(1)} %get-tuple-element.11.queries, f32[4,192,16]{2,1,0:T(8,128)S(1)} %get-tuple-element.12.unseen, bf16[128,256]{1,0:T(8,128)(2,1)S(1)} %get-tuple-element.13.chosen, ...), custom_call_target="tpu_custom_call" | custom-call | tf_op jit(solution)/shard_map/projected/pallas_call | solution.py:463
  43.4 16.1 %all_to_all.17.received = bf16[8,96,256]{2,1,0:T(8,128)(2,1)S(1)} all-to-all(bf16[8,96,256]{2,1,0:T(8,128)(2,1)S(1)} %projected.1), channel_id=1, replica_groups=mesh['seq'=32,'tp'=8] {'tp'}, dimensions={0} | all-to-all | bytes 786432 | tf_op jit(solution)/shard_map/all_to_all | solution.py:471
  59.5 0.8 %summed.1 = bf16[3,2,16,256]{3,2,1,0:T(8,128)(2,1)} custom-call(bf16[8,96,256]{2,1,0:T(8,128)(2,1)S(1)} %all_to_all.17.received, bf16[96,96]{1,0:T(8,128)(2,1)S(1)} %get-tuple-element.14.gather), custom_call_target="tpu_custom_call" | custom-call | tf_op jit(solution)/shard_map/summed/pallas_call | solution.py:472
Async XLA Ops:
  0.0 42.3 %copy-start = (bf16[1024,256]{1,0:T(8,128)(2,1)S(1)}, bf16[1024,256]{1,0:T(8,128)(2,1)}, u32[]{:S(2)}) copy-start(bf16[1024,256]{1,0:T(8,128)(2,1)} %w_out.1) | copy-start | bytes 1572868
